TPU v7x, 128 devices: a whole 4x4x4 slice. The times are simulated.
128 devices in a mesh: gx: 8 (over z_lo, x), gy: 16 (over z_hi, y, core).
Axes of the slice: x: 4, y: 4, z: 4 (z_hi: 2, z_lo: 2; z = z_hi * 2 + z_lo), core: 2. Of those that a mesh axis runs over, the one named last changes fastest.
Arguments:
- samples: bfloat16 [1024, 262144], P(('gx', 'gy')), may hold values from -6 to 6
- interp: bfloat16 [2, 2048, 32, 128], P(None, ('gx', 'gy')), may hold values from -0.5 to 0.5
- translation: bfloat16 [7, 2, 2048, 32, 64], P(None, None, ('gx', 'gy')), may hold values from -0.5 to 0.5
- evaluate: bfloat16 [2, 262144, 32], P(None, ('gx', 'gy')), may hold values from -0.75 to 0.75
Outputs:
- radon: float32 [1024, 262144], P(None, ('gx', 'gy'))
All inputs are finite; a program needn't handle non-finite values.
Results may differ from a plain program's by a relative error of at most 0.013.
Values may be sent and summed in bfloat16 or wider, within the bound.
A program may use at most 128 MiB of HBM per device.

v0:
```python
import jax
import jax.numpy as jnp
from jax import lax
from jax.sharding import PartitionSpec as P


def partner_2(block, axis, stride):
    count = lax.axis_size(axis)
    route = []
    for low in range(count):
        high = low | 1 << stride
        if high != low and high < count:
            route += [(low, high), (high, low)]
    return lax.ppermute(block, axis, route)


def box_product(weight, values):
    return jnp.einsum("bkj,bjr->bkr", weight, values, preferred_element_type=jnp.float32)


def advance(state, partner, weight):
    stacked = jnp.concatenate([state, partner], axis=2)
    real = box_product(weight[0], stacked[0]) - box_product(weight[1], stacked[1])
    imag = box_product(weight[0], stacked[1]) + box_product(weight[1], stacked[0])
    return jnp.stack([real, imag]).astype(jnp.bfloat16)


def on_device(samples, interp, translation, evaluate):
    gathered = lax.all_to_all(samples, ("gx", "gy"), split_axis=1, concat_axis=0, tiled=True)
    box_count = interp.shape[1]
    records = gathered.shape[0]
    by_box = gathered.reshape(records, box_count, interp.shape[3])
    state = jnp.einsum("cbks,rbs->cbkr", interp, by_box, preferred_element_type=jnp.float32).astype(
        jnp.bfloat16
    )
    bits_low = lax.axis_size("gy").bit_length() - 1
    bits_high = lax.axis_size("gx").bit_length() - 1
    level = 0
    for bit in range(bits_low):
        partner = partner_2(state, "gy", bit)
        state = advance(state, partner, translation[level])
        level = level + 1
    for bit in range(bits_high):
        partner = partner_2(state, "gx", bit)
        state = advance(state, partner, translation[level])
        level = level + 1
    table = evaluate.reshape(2, box_count, evaluate.shape[1] // box_count, evaluate.shape[2])
    result = jnp.einsum("btk,bkr->rbt", table[0], state[0], preferred_element_type=jnp.float32)
    result = result - jnp.einsum(
        "btk,bkr->rbt", table[1], state[1], preferred_element_type=jnp.float32
    )
    return result.reshape(records, evaluate.shape[1])


def solution(mesh):
    in_specs = (
        P(("gx", "gy"), None),
        P(None, ("gx", "gy"), None, None),
        P(None, None, ("gx", "gy"), None, None),
        P(None, ("gx", "gy"), None),
    )
    out_specs = P(None, ("gx", "gy"))
    return jax.shard_map(
        on_device, mesh=mesh, in_specs=in_specs, out_specs=out_specs, check_vma=False
    )
```

profile of v0, /device:TPU:1, one launch (start us, length us, event | category | flops | bytes accessed | tf_op | source)
XLA Modules:
  0.0 394.5 jit_solution(262456761446602728)
XLA Ops:
  0.0 68.0 %all_to_all.16 = bf16[8,128,2048]{2,0,1:T(8,128)(2,1)S(1)} all-to-all(bf16[8,128,2048]{2,0,1:T(8,128)(2,1)} %bitcast.250), channel_id=1, replica_groups=mesh['gx'=8,'gy'=16] {'gx','gy'}, dimensions={1} | all-to-all | bytes 8388608 | tf_op jit(solution)/shard_map/all_to_all | solution.py:29
  68.0 1.4 copy.15
  69.5 2.6 convert_bitcast_fusion
  72.2 4.1 %collective-permute-done = bf16[2,16,32,1024]{3,2,0,1:T(8,128)(2,1)S(1)} collective-permute-done((bf16[2,16,32,1024]{3,2,0,1:T(8,128)(2,1)S(1)}, bf16[2,16,32,1024]{3,2,0,1:T(8,128)(2,1)S(1)}, u32[]{:S(2)}, u32[]{:S(2)}) %collective-permute-start) | collective-permute-done | bytes 2097184 | tf_op jit(solution)/shard_map/ppermute | solution.py:14
  77.2 0.5 fusion.31
  78.4 47.1 %collective-permute-done.1 = bf16[2,16,32,1024]{3,2,1,0:T(8,128)(2,1)S(1)} collective-permute-done((bf16[2,16,32,1024]{3,2,1,0:T(8,128)(2,1)S(1)}, bf16[2,16,32,1024]{3,2,1,0:T(8,128)(2,1)S(1)}, u32[]{:S(2)}, u32[]{:S(2)}) %collective-permute-start.1) | collective-permute-done | bytes 2097184 | tf_op jit(solution)/shard_map/ppermute | solution.py:14
  125.5 0.5 pad_maximum_fusion
  126.8 0.5 fusion.33
  127.3 0.5 fusion.34
  128.1 47.7 %collective-permute-done.2 = bf16[2,16,32,1024]{3,2,1,0:T(8,128)(2,1)S(1)} collective-permute-done((bf16[2,16,32,1024]{3,2,1,0:T(8,128)(2,1)S(1)}, bf16[2,16,32,1024]{3,2,1,0:T(8,128)(2,1)S(1)}, u32[]{:S(2)}, u32[]{:S(2)}) %collective-permute-start.2) | collective-permute-done | bytes 2097184 | tf_op jit(solution)/shard_map/ppermute | solution.py:14
  175.8 0.5 pad_maximum_fusion.1
  177.2 0.5 fusion.35
  177.7 0.5 fusion.36
  178.6 46.7 %collective-permute-done.3 = bf16[2,16,32,1024]{3,2,1,0:T(8,128)(2,1)S(1)} collective-permute-done((bf16[2,16,32,1024]{3,2,1,0:T(8,128)(2,1)S(1)}, bf16[2,16,32,1024]{3,2,1,0:T(8,128)(2,1)S(1)}, u32[]{:S(2)}, u32[]{:S(2)}) %collective-permute-start.3) | collective-permute-done | bytes 2097184 | tf_op jit(solution)/shard_map/ppermute | solution.py:14
  225.4 0.5 pad_maximum_fusion.2
  226.8 0.5 fusion.37
  227.3 0.5 fusion.38
  228.1 44.3 %collective-permute-done.4 = bf16[2,16,32,1024]{3,2,1,0:T(8,128)(2,1)S(1)} collective-permute-done((bf16[2,16,32,1024]{3,2,1,0:T(8,128)(2,1)S(1)}, bf16[2,16,32,1024]{3,2,1,0:T(8,128)(2,1)S(1)}, u32[]{:S(2)}, u32[]{:S(2)}) %collective-permute-start.4) | collective-permute-done | bytes 2097184 | tf_op jit(solution)/shard_map/ppermute | solution.py:14
  272.4 0.5 pad_maximum_fusion.3
  273.7 0.5 fusion.39
  274.2 0.5 fusion.40
  275.0 44.9 %collective-permute-done.5 = bf16[2,16,32,1024]{3,2,1,0:T(8,128)(2,1)S(1)} collective-permute-done((bf16[2,16,32,1024]{3,2,1,0:T(8,128)(2,1)S(1)}, bf16[2,16,32,1024]{3,2,1,0:T(8,128)(2,1)S(1)}, u32[]{:S(2)}, u32[]{:S(2)}) %collective-permute-start.5) | collective-permute-done | bytes 2097184 | tf_op jit(solution)/shard_map/ppermute | solution.py:14
  319.9 0.5 pad_maximum_fusion.4
  321.3 0.5 fusion.41
  321.8 0.5 fusion.42
  323.3 41.8 %collective-permute-done.6 = bf16[2,16,32,1024]{3,2,1,0:T(8,128)(2,1)S(1)} collective-permute-done((bf16[2,16,32,1024]{3,2,1,0:T(8,128)(2,1)S(1)}, bf16[2,16,32,1024]{3,2,1,0:T(8,128)(2,1)S(1)}, u32[]{:S(2)}, u32[]{:S(2)}) %collective-permute-start.6) | collective-permute-done | bytes 2097184 | tf_op jit(solution)/shard_map/ppermute | solution.py:14
  365.1 0.5 pad_maximum_fusion.5
  366.0 1.5 copy-done.2
  367.5 1.7 fusion.28
  369.3 6.6 %fusion.43 = f32[16,1024,128]{1,2,0:T(8,128)} fusion(f32[16,1024,32]{1,2,0:T(8,128)S(1)} %fusion.29, bf16[2,16,64,1024]{3,2,1,0:T(8,128)(2,1)} %copy-done.2, bf16[16,128,32]{1,0,2:T(8,128)(2,1)S(1)} %bitcast.252, bf16[7,2,16,32,64]{4,3,2,1,0:T(8,128)(2,1)} %param.6), kind=kOutput, calls=%fused_computation.84 | convolution fusion | flops 202375168 | bytes 12845056 | tf_op jit(solution)/shard_map/btk,bkr->rbt/dot_general | solution.py:48
  375.9 9.4 %convolution_subtract_fusion = f32[16,1024,128]{1,2,0:T(8,128)} fusion(f32[16,1024,128]{1,2,0:T(8,128)} %fusion.43, f32[16,1024,32]{1,2,0:T(8,128)} %fusion.28, bf16[2,16,64,1024]{3,2,1,0:T(8,128)(2,1)} %copy-done.2, bf16[16,128,32]{1,0,2:T(8,128)(2,1)S(1)} %bitcast.253, bf16[7,2,16,32,64]{4,3,2,1,0:T(8,128)(2,1)} %param.6), kind=kOutput, calls=%fused_computation.10 | convolution fusion | flops 204472320 | bytes 21233664 | tf_op jit(solution)/shard_map/btk,bkr->rbt/dot_general | solution.py:49
  385.3 9.2 %copy.11 = f32[1024,2048]{1,0:T(8,128)} copy(f32[1024,2048]{0,1:T(8,128)} %bitcast.248) | data formatting | bytes 16777216 | tf_op jit(solution)/shard_map/reshape | solution.py:52
  (39 shorter events, 8.7 us)
Async XLA Ops:
  0.0 69.4 %copy-start = (bf16[2,16,32,128]{3,2,1,0:T(8,128)(2,1)S(1)}, bf16[2,16,32,128]{3,2,1,0:T(8,128)(2,1)}, u32[]{:S(2)}) copy-start(bf16[2,16,32,128]{3,2,1,0:T(8,128)(2,1)} %param.5) | copy-start | bytes 786436
  69.4 6.9 %copy-start.3 = (bf16[7,2,16,32,64]{4,3,2,1,0:T(8,128)(2,1)S(1)}, bf16[7,2,16,32,64]{4,3,2,1,0:T(8,128)(2,1)}, u32[]{:S(2)}) copy-start(bf16[7,2,16,32,64]{4,3,2,1,0:T(8,128)(2,1)} %param.6) | copy-start | bytes 2752516
  72.1 4.2 %collective-permute-start = (bf16[2,16,32,1024]{3,2,0,1:T(8,128)(2,1)S(1)}, bf16[2,16,32,1024]{3,2,0,1:T(8,128)(2,1)S(1)}, u32[]{:S(2)}, u32[]{:S(2)}) collective-permute-start(bf16[2,16,32,1024]{3,2,0,1:T(8,128)(2,1)S(1)} %convert_bitcast_fusion), channel_id=1, source_target_pairs={{0,1},{1,0},{2,3},{3,2},{4,5},{5,4},{6,7},{7,6},{8,9},{9,8},{10,11... | collective-permute-start | bytes 6291464 | tf_op jit(solution)/shard_map/ppermute | solution.py:14
  78.3 47.2 %collective-permute-start.1 = (bf16[2,16,32,1024]{3,2,1,0:T(8,128)(2,1)S(1)}, bf16[2,16,32,1024]{3,2,1,0:T(8,128)(2,1)S(1)}, u32[]{:S(2)}, u32[]{:S(2)}) collective-permute-start(bf16[2,16,32,1024]{3,2,1,0:T(8,128)(2,1)S(1)} %pad_maximum_fusion.7), channel_id=1, source_target_pairs={{0,2},{2,0},{1,3},{3,1},{4,6},{6,4},{5,7},{7,5},{8,10},{10,8},{9,1... | collective-permute-start | bytes 6291464 | tf_op jit(solution)/shard_map/ppermute | solution.py:14
  128.0 47.8 %collective-permute-start.2 = (bf16[2,16,32,1024]{3,2,1,0:T(8,128)(2,1)S(1)}, bf16[2,16,32,1024]{3,2,1,0:T(8,128)(2,1)S(1)}, u32[]{:S(2)}, u32[]{:S(2)}) collective-permute-start(bf16[2,16,32,1024]{3,2,1,0:T(8,128)(2,1)S(1)} %pad_maximum_fusion.8), channel_id=1, source_target_pairs={{0,4},{4,0},{1,5},{5,1},{2,6},{6,2},{3,7},{7,3},{8,12},{12,8},{9,1... | collective-permute-start | bytes 6291464 | tf_op jit(solution)/shard_map/ppermute | solution.py:14
  178.4 47.0 %collective-permute-start.3 = (bf16[2,16,32,1024]{3,2,1,0:T(8,128)(2,1)S(1)}, bf16[2,16,32,1024]{3,2,1,0:T(8,128)(2,1)S(1)}, u32[]{:S(2)}, u32[]{:S(2)}) collective-permute-start(bf16[2,16,32,1024]{3,2,1,0:T(8,128)(2,1)S(1)} %pad_maximum_fusion.9), channel_id=1, source_target_pairs={{0,8},{8,0},{1,9},{9,1},{2,10},{10,2},{3,11},{11,3},{4,12},{12,4},... | collective-permute-start | bytes 6291464 | tf_op jit(solution)/shard_map/ppermute | solution.py:14
  228.0 44.4 %collective-permute-start.4 = (bf16[2,16,32,1024]{3,2,1,0:T(8,128)(2,1)S(1)}, bf16[2,16,32,1024]{3,2,1,0:T(8,128)(2,1)S(1)}, u32[]{:S(2)}, u32[]{:S(2)}) collective-permute-start(bf16[2,16,32,1024]{3,2,1,0:T(8,128)(2,1)S(1)} %pad_maximum_fusion.10), channel_id=1, source_target_pairs={{0,16},{16,0},{32,48},{48,32},{64,80},{80,64},{96,112},{112,96},{1... | collective-permute-start | bytes 6291464 | tf_op jit(solution)/shard_map/ppermute | solution.py:14
  274.9 45.0 %collective-permute-start.5 = (bf16[2,16,32,1024]{3,2,1,0:T(8,128)(2,1)S(1)}, bf16[2,16,32,1024]{3,2,1,0:T(8,128)(2,1)S(1)}, u32[]{:S(2)}, u32[]{:S(2)}) collective-permute-start(bf16[2,16,32,1024]{3,2,1,0:T(8,128)(2,1)S(1)} %pad_maximum_fusion.11), channel_id=1, source_target_pairs={{0,32},{32,0},{16,48},{48,16},{64,96},{96,64},{80,112},{112,80},{1... | collective-permute-start | bytes 6291464 | tf_op jit(solution)/shard_map/ppermute | solution.py:14
  322.3 1.0 copy-start.4
  322.5 42.6 %collective-permute-start.6 = (bf16[2,16,32,1024]{3,2,1,0:T(8,128)(2,1)S(1)}, bf16[2,16,32,1024]{3,2,1,0:T(8,128)(2,1)S(1)}, u32[]{:S(2)}, u32[]{:S(2)}) collective-permute-start(bf16[2,16,32,1024]{3,2,1,0:T(8,128)(2,1)S(1)} %pad_maximum_fusion.12), channel_id=1, source_target_pairs={{0,64},{64,0},{16,80},{80,16},{32,96},{96,32},{48,112},{112,48},{1... | collective-permute-start | bytes 6291464 | tf_op jit(solution)/shard_map/ppermute | solution.py:14
  365.6 2.0 copy-start.2
  385.3 9.2 %copy-start.1 = (bf16[2,16,32,128]{3,2,1,0:T(8,128)(2,1)S(1)}, bf16[2,16,32,128]{3,2,1,0:T(8,128)(2,1)}, u32[]{:S(2)}) copy-start(bf16[2,16,32,128]{3,2,1,0:T(8,128)(2,1)} %param.5) | copy-start | bytes 786436
where the time goes:
time: 399 us; the launch traced here: 394 us
  waiting for transfers between devices  277 us (69%)
  blocking collectives  68 us (17%)
  matrix products  31.9 us (8%)
  local copies, waits for them, and re-layouts  12.6 us (3%)
  other arithmetic  4.05 us (1%)
    ppermute x7, waiting for transfers between devices, partner_2(): return lax.ppermute(block, axis, route)  277 us
    all_to_all x1, blocking collectives, on_device(): lax.all_to_all(samples, ('gx', 'gy'), split_axis=1, concat_axis=0, tiled=...  68 us
    dot_general x26, matrix products, box_product(): jnp.einsum('bkj,bjr->bkr', weight, values, preferred_element_type=jnp.flo...  13.2 us
    dot_general x1, matrix products, on_device(): jnp.einsum('btk,bkr->rbt', table[1], state[1], preferred_element_type=jnp...  9.44 us
    reshape x1, local copies, waits for them, and re-layouts, on_device(): return result.reshape(records, evaluate.shape[1])  9.17 us
  transfers between devices with their start and end apart: 7, of which 7 were waited for; matrix products, arithmetic and copies ran while one was open for 0% of the time, Pallas kernels for 0%

commit v1 on v0

v1 whole, which is shorter than its diff:
```python
import jax
import jax.numpy as jnp
from jax import lax
from jax.experimental import pallas as pl
from jax.experimental.pallas import tpu as pltpu
from jax.sharding import PartitionSpec as P

MESH = pl.DeviceIdType.MESH
F32, BF16 = jnp.float32, jnp.bfloat16
ANY = pl.BlockSpec(memory_space=pl.ANY)
LIMIT = 56 * 2**20


def place():
    return lax.axis_index("gx"), lax.axis_index("gy")


def greet(devices):
    barrier = pltpu.get_barrier_semaphore()
    for device in devices:
        pl.semaphore_signal(barrier, inc=1, device_id=device, device_id_type=MESH)
    pl.semaphore_wait(barrier, len(devices))


def spread_kernel(samples, own_w, own_v, x, w, v, send, recv, here):
    gx, gy = place()
    y = (gy >> 1) & 3
    up = (gy & 9) | (((y + 1) & 3) << 1)
    down = (gy & 9) | (((y + 3) & 3) << 1)
    far = gy ^ 8
    core = gy ^ 1
    greet([(gx, up), (gx, down), (gx, far), (gx, core)] + [(gx ^ m, gy) for m in range(1, 8)])
    used = [0]

    def push(src, dst, device):
        k = used[0]
        used[0] = k + 1
        copy = pltpu.make_async_remote_copy(
            src_ref=src, dst_ref=dst, send_sem=send.at[k], recv_sem=recv.at[k],
            device_id=device, device_id_type=MESH)
        copy.start()
        return copy

    keep = [pltpu.make_async_copy(samples.at[gx], x.at[gx], here.at[0]),
            pltpu.make_async_copy(own_w, w.at[gy], here.at[1]),
            pltpu.make_async_copy(own_v, v.at[gx], here.at[2])]
    to_far = push(own_w, w.at[gy], (gx, far))
    to_up = push(own_w, w.at[gy], (gx, up))
    to_down = push(own_w, w.at[gy], (gx, down))
    sent = [push(samples.at[gx ^ m], x.at[gx], (gx ^ m, gy)) for m in range(1, 8)]
    to_core = [push(own_w, w.at[gy], (gx, core))]
    for copy in keep:
        copy.start()
    lo, hi = pl.ds(0, 8), pl.ds(8, 8)

    def relay(from_down, from_up, flip):
        a, b = down ^ flip, up ^ flip
        from_down.wait_recv()
        one = push(w.at[a, lo], w.at[a, lo], (gx, up))
        core_a = push(w.at[a], w.at[a], (gx, core))
        from_up.wait_recv()
        two = push(w.at[b, hi], w.at[b, hi], (gx, down))
        core_b = push(w.at[b], w.at[b], (gx, core))
        return [one, two], [core_a, core_b]

    halves, cores = relay(to_up, to_down, 0)
    to_core += cores
    to_far.wait_recv()
    far_up = push(w.at[far], w.at[far], (gx, up))
    far_down = push(w.at[far], w.at[far], (gx, down))
    to_core.append(push(w.at[far], w.at[far], (gx, core)))
    own_4 = push(own_v, v.at[gx], (gx ^ 4, gy))
    own_x = [push(own_v, v.at[gx], (gx ^ m, gy)) for m in (1, 2, 3)]
    far_halves, cores = relay(far_up, far_down, 8)
    to_core += cores
    own_4.wait_recv()
    mate = gx ^ 4
    next_x = [push(v.at[mate], v.at[mate], (gx ^ m, gy)) for m in (1, 2, 3)]
    for flip, pair in ((0, halves), (8, far_halves)):
        for copy in pair:
            copy.wait_recv()
        opposite = gy ^ 4 ^ flip
        to_core.append(push(w.at[opposite], w.at[opposite], (gx, core)))
    for copy in sent + to_core + own_x + next_x:
        copy.wait()
    for copy in [to_far, to_up, to_down, far_up, far_down, own_4] + halves + far_halves:
        copy.wait_send()
    for copy in keep:
        copy.wait()


def spread(samples, own_w, own_v):
    return pl.pallas_call(
        spread_kernel,
        out_shape=[jax.ShapeDtypeStruct(samples.shape, BF16),
                   jax.ShapeDtypeStruct((16,) + own_w.shape, BF16),
                   jax.ShapeDtypeStruct((8,) + own_v.shape, BF16)],
        in_specs=[ANY] * 3,
        out_specs=[ANY] * 3,
        scratch_shapes=[pltpu.SemaphoreType.DMA((40,)), pltpu.SemaphoreType.DMA((40,)),
                        pltpu.SemaphoreType.DMA((3,))],
        compiler_params=pltpu.CompilerParams(collective_id=1, has_side_effects=True),
        name="spread",
    )(samples, own_w, own_v)


def turn(pair, first):
    moved = pltpu.roll(pair, 64, 1)
    return jnp.where(first, -moved, moved).astype(BF16)


def low_kernel(x_ref, w_ref, o_ref, state, turned):
    first = lax.broadcasted_iota(jnp.int32, (32, 128), 1) < 64
    for g in range(16):
        rows = x_ref[:, g, 0].reshape(64, 128)
        table = w_ref[g, 0, 0:2].reshape(64, 128)
        got = lax.dot_general(table, rows, (((1,), (1,)), ((), ())), preferred_element_type=F32)
        pair = jnp.concatenate([got[:32], got[32:]], axis=1)
        state[0, g] = pair.astype(BF16)
        turned[0, g] = turn(pair, first)
    for level in range(4):
        now, later = level % 2, (level + 1) % 2
        for g in range(16):
            h = g ^ (1 << level)
            right = jnp.concatenate(
                [state[now, g], state[now, h], turned[now, g], turned[now, h]], axis=0)
            got = jnp.dot(w_ref[g, 0, 2 + level], right, preferred_element_type=F32)
            if level == 3:
                o_ref[g, 0] = got.astype(BF16)
            else:
                state[later, g] = got.astype(BF16)
                turned[later, g] = turn(got, first)


def low(x, w):
    return pl.pallas_call(
        low_kernel,
        grid=(16,),
        out_shape=jax.ShapeDtypeStruct((16, 16, 32, 128), BF16),
        in_specs=[pl.BlockSpec((8, 16, 1, 8, 128), lambda b: (0, 0, b, 0, 0)),
                  pl.BlockSpec((16, 1, 6, 32, 128), lambda b: (0, b, 0, 0, 0))],
        out_specs=pl.BlockSpec((16, 1, 32, 128), lambda b: (0, (b % 8) * 2 + b // 8, 0, 0)),
        scratch_shapes=[pltpu.VMEM((2, 16, 32, 128), BF16), pltpu.VMEM((2, 16, 32, 128), BF16)],
        compiler_params=pltpu.CompilerParams(vmem_limit_bytes=LIMIT),
        name="low",
    )(x, w)


def swap_kernel(o, t, send, recv, here):
    gx, gy = place()
    half = gy & 1
    barrier = pltpu.get_barrier_semaphore()

    def hello(m, carry):
        pl.semaphore_signal(
            barrier, inc=1, device_id=(gx ^ (m >> 4), gy ^ (m & 15)), device_id_type=MESH)
        return carry

    lax.fori_loop(1, 128, hello, 0)
    pl.semaphore_wait(barrier, 127)

    def copy(m):
        gx2, gy2 = gx ^ (m >> 4), gy ^ (m & 15)
        j = gx2 ^ (gy >> 1)
        return pltpu.make_async_remote_copy(
            src_ref=o.at[gy2, j], dst_ref=t.at[gx, j, half], send_sem=send.at[m],
            recv_sem=recv.at[m], device_id=(gx2, gy2), device_id_type=MESH)

    def start(m, carry):
        copy(m).start()
        return carry

    def finish(m, carry):
        copy(m).wait()
        return carry

    lax.fori_loop(1, 128, start, 0)
    j = gx ^ (gy >> 1)
    keep = pltpu.make_async_copy(o.at[gy, j], t.at[gx, j, half], here)
    keep.start()
    lax.fori_loop(1, 128, finish, 0)
    keep.wait()


def swap(o):
    return pl.pallas_call(
        swap_kernel,
        out_shape=jax.ShapeDtypeStruct((8, 8, 2, 2, 32, 128), BF16),
        in_specs=[ANY],
        out_specs=ANY,
        scratch_shapes=[pltpu.SemaphoreType.DMA((128,)), pltpu.SemaphoreType.DMA((128,)),
                        pltpu.SemaphoreType.DMA],
        compiler_params=pltpu.CompilerParams(collective_id=2, has_side_effects=True),
        name="swap",
    )(o.reshape(16, 8, 2, 32, 128))


def high_kernel(t_ref, v_ref, f_ref, state, turned):
    first = lax.broadcasted_iota(jnp.int32, (32, 128), 1) < 64
    for g in range(8):
        for half in range(2):
            tile = t_ref[g, 0, half, 0]
            state[0, g, :, half * 128:half * 128 + 128] = tile
            turned[0, g, :, half * 128:half * 128 + 128] = turn(tile.astype(F32), first)
    for level in range(3):
        now, later = level % 2, (level + 1) % 2
        for g in range(8):
            h = g ^ (1 << level)
            right = jnp.concatenate(
                [state[now, g], state[now, h], turned[now, g], turned[now, h]], axis=0)
            got = jnp.dot(v_ref[g, 0, level], right, preferred_element_type=F32)
            one, two = got[:, :128], got[:, 128:]
            if level == 2:
                f_ref[g, 0, 0] = jnp.where(first, one, pltpu.roll(two, 64, 1)).astype(BF16)
                f_ref[g, 0, 1] = jnp.where(first, pltpu.roll(one, 64, 1), two).astype(BF16)
            else:
                state[later, g] = got.astype(BF16)
                turned[later, g, :, :128] = turn(one, first)
                turned[later, g, :, 128:] = turn(two, first)


def high(t, v):
    return pl.pallas_call(
        high_kernel,
        grid=(16,),
        out_shape=jax.ShapeDtypeStruct((8, 16, 2, 32, 128), BF16),
        in_specs=[pl.BlockSpec((8, 1, 2, 1, 32, 128), lambda i: (0, i // 2, 0, i % 2, 0, 0)),
                  pl.BlockSpec((8, 1, 3, 32, 128), lambda i: (0, i // 2 + (i % 2) * 8, 0, 0, 0))],
        out_specs=pl.BlockSpec((8, 1, 2, 32, 128), lambda i: (0, i, 0, 0, 0)),
        scratch_shapes=[pltpu.VMEM((2, 8, 32, 256), BF16), pltpu.VMEM((2, 8, 32, 256), BF16)],
        compiler_params=pltpu.CompilerParams(vmem_limit_bytes=LIMIT),
        name="high",
    )(t, v)


def home_kernel(f, g, send, recv, here):
    gx, gy = place()
    greet([(gx ^ m, gy) for m in range(1, 8)])
    copies = [
        pltpu.make_async_remote_copy(
            src_ref=f.at[gx ^ m], dst_ref=g.at[gx], send_sem=send.at[m], recv_sem=recv.at[m],
            device_id=(gx ^ m, gy), device_id_type=MESH)
        for m in range(1, 8)]
    for copy in copies:
        copy.start()
    keep = pltpu.make_async_copy(f.at[gx], g.at[gx], here)
    keep.start()
    for copy in copies:
        copy.wait()
    keep.wait()


def home(f):
    return pl.pallas_call(
        home_kernel,
        out_shape=jax.ShapeDtypeStruct(f.shape, BF16),
        in_specs=[ANY],
        out_specs=ANY,
        scratch_shapes=[pltpu.SemaphoreType.DMA((8,)), pltpu.SemaphoreType.DMA((8,)),
                        pltpu.SemaphoreType.DMA],
        compiler_params=pltpu.CompilerParams(collective_id=3, has_side_effects=True),
        name="home",
    )(f)


def last_kernel(g_ref, e_ref, r_ref):
    j = pl.program_id(0) // 2
    table = jnp.concatenate([e_ref[0], -e_ref[1]], axis=0)
    for s in range(8):
        left = g_ref[s, 0].reshape(64, 128)
        got = lax.dot_general(
            left, table, (((0,), (0,)), ((), ())), preferred_element_type=F32)
        got = got.reshape(2, 8, 8, 128)
        for half in range(2):
            r_ref[:, 2 * (s ^ j) + half] = got[half]


def last(g, e):
    return pl.pallas_call(
        last_kernel,
        grid=(16,),
        out_shape=jax.ShapeDtypeStruct((8, 16, 8, 2048), F32),
        in_specs=[pl.BlockSpec((8, 1, 2, 32, 128), lambda i: (0, i, 0, 0, 0)),
                  pl.BlockSpec((2, 32, 128), lambda i: (0, 0, i // 2 + (i % 2) * 8))],
        out_specs=pl.BlockSpec((8, 16, 8, 128), lambda i: (0, 0, 0, i // 2 + (i % 2) * 8)),
        compiler_params=pltpu.CompilerParams(vmem_limit_bytes=LIMIT),
        name="last",
    )(g, e)


def on_device(samples, interp, translation, evaluate):
    by_box = samples.reshape(8, 2048, 128).transpose(1, 0, 2).reshape(8, 16, 16, 8, 128)
    levels = translation.transpose(2, 0, 3, 1, 4).reshape(16, 7, 32, 128)
    own_w = jnp.concatenate([interp.transpose(1, 0, 2, 3), levels[:, :4]], axis=1)
    own_v = levels[:, 4:]
    x, w, v = spread(by_box, own_w, own_v)
    state = home(high(swap(low(x, w)), v))
    return last(state, evaluate.transpose(0, 2, 1)).reshape(1024, 2048)


def solution(mesh):
    in_specs = (
        P(("gx", "gy"), None),
        P(None, ("gx", "gy"), None, None),
        P(None, None, ("gx", "gy"), None, None),
        P(None, ("gx", "gy"), None),
    )
    out_specs = P(None, ("gx", "gy"))
    return jax.shard_map(
        on_device, mesh=mesh, in_specs=in_specs, out_specs=out_specs, check_vma=False
    )
```

time: 399 us -> 230 us (0.58); the launches traced: 394 us -> 230 us
  waiting for transfers between devices: 277 us -> 0 us
  Pallas kernels: 0 us -> 222 us
  blocking collectives: 68 us -> 0 us
  matrix products: 31.9 us -> 0 us
  local copies, waits for them, and re-layouts: 12.6 us -> 6.97 us
    ppermute x7 -> x0, waiting for transfers between devices: 277 us -> none  [partner_2(): return lax.ppermute(block, axis, route)]
    pallas_call x0 -> x6, Pallas kernels: none -> 222 us  [the longest x1 96.7 us: spread(): pl.pallas_call(spread_kernel, out_shape=[jax.ShapeDtypeStruct(samples.sha...]
    all_to_all x1 -> x0, blocking collectives: 68 us -> none  [on_device(): lax.all_to_all(samples, ('gx', 'gy'), split_axis=1, concat_axis=0, tiled=...]
    dot_general x29 -> x0, matrix products: 31.9 us -> none  [the longest x26 13.2 us: box_product(): jnp.einsum('bkj,bjr->bkr', weight, values, preferred_element_type=jnp.flo...]
    reshape x1, local copies, waits for them, and re-layouts: 9.17 us -> 0.83 us  [on_device(): levels = translation.transpose(2, 0, 3, 1, 4).reshape(16, 7, 32, 128)]
    transpose x0 -> x1, local copies, waits for them, and re-layouts: none -> 4.35 us  [on_device(): levels = translation.transpose(2, 0, 3, 1, 4).reshape(16, 7, 32, 128)]
  transfers between devices with their start and end apart: 7 -> 0, of which waited for: 7 -> 0; matrix products, arithmetic and copies ran while one was open for 0% -> 0% of each run, Pallas kernels for 0% -> 0%
where the time goes in v1:
time: 230 us
  Pallas kernels  222 us (97%)
  local copies, waits for them, and re-layouts  6.97 us (3%)
    pallas_call x1, Pallas kernels, spread(): pl.pallas_call(spread_kernel, out_shape=[jax.ShapeDtypeStruct(samples.sha...  96.7 us
    pallas_call x1, Pallas kernels, swap(): pl.pallas_call(swap_kernel, out_shape=jax.ShapeDtypeStruct((8, 8, 2, 2, 3...  40.1 us
    pallas_call x1, Pallas kernels, home(): pl.pallas_call(home_kernel, out_shape=jax.ShapeDtypeStruct(f.shape, BF16)...  31.1 us
    pallas_call x1, Pallas kernels, low(): pl.pallas_call(low_kernel, grid=(16,), out_shape=jax.ShapeDtypeStruct((16...  24.4 us
    pallas_call x1, Pallas kernels, high(): pl.pallas_call(high_kernel, grid=(16,), out_shape=jax.ShapeDtypeStruct((8...  17.1 us
    pallas_call x1, Pallas kernels, last(): pl.pallas_call(last_kernel, grid=(16,), out_shape=jax.ShapeDtypeStruct((8...  12.3 us

profile of v1, /device:TPU:1, one launch (start us, length us, event | category | flops | bytes accessed | tf_op | source)
XLA Modules:
  0.0 229.6 jit_solution(12464100256358203380)
XLA Ops:
  0.0 1.0 copy.8
  1.0 4.4 %copy.6 = bf16[16,7,32,2,64]{4,3,2,1,0:T(2,128)(2,1)S(1)} copy(bf16[16,7,32,2,64]{4,2,0,3,1:T(8,128)(2,1)} %bitcast.14) | data formatting | bytes 1835008 | tf_op jit(solution)/shard_map/transpose | solution.py:293
  5.3 0.8 reshape.17
  6.2 0.8 slice.9.own_v
  7.0 1.0 pad_maximum_fusion.own_w
  8.0 96.7 %spread.1 = (bf16[8,16,16,8,128]{4,3,2,1,0:T(8,128)(2,1)}, bf16[16,16,6,32,128]{4,3,2,1,0:T(8,128)(2,1)}, bf16[8,16,3,32,128]{4,3,2,1,0:T(8,128)(2,1)}) custom-call(bf16[8,16,16,8,128]{4,3,2,1,0:T(8,128)(2,1)} %bitcast.13, bf16[16,6,32,128]{3,2,1,0:T(8,128)(2,1)} %pad_maximum_fusion.own_w, bf16[16,3,32,128]{3,2,1,0:T(8,128)(2,1)} %slice.9.own_v), custom_call_target="tpu_custom_call" | custom-call | tf_op jit(solution)/shard_map/spread/pallas_call | solution.py:93
  104.7 24.4 %low.1 = bf16[16,16,32,128]{3,2,1,0:T(8,128)(2,1)} custom-call(bf16[8,16,16,8,128]{4,3,2,1,0:T(8,128)(2,1)} %get-tuple-element.8.x_ref, bf16[16,16,6,32,128]{4,3,2,1,0:T(8,128)(2,1)} %get-tuple-element.9.w_ref), custom_call_target="tpu_custom_call" | custom-call | tf_op jit(solution)/shard_map/low/pallas_call | solution.py:136
  129.1 40.1 %swap.1.t_ref = bf16[8,8,2,2,32,128]{5,4,3,2,1,0:T(8,128)(2,1)} custom-call(bf16[16,8,2,32,128]{4,3,2,1,0:T(8,128)(2,1)} %bitcast.12), custom_call_target="tpu_custom_call" | custom-call | tf_op jit(solution)/shard_map/swap/pallas_call | solution.py:186
  169.2 17.1 %high.1.f = bf16[8,16,2,32,128]{4,3,2,1,0:T(8,128)(2,1)} custom-call(bf16[8,8,2,2,32,128]{5,4,3,2,1,0:T(8,128)(2,1)} %swap.1.t_ref, bf16[8,16,3,32,128]{4,3,2,1,0:T(8,128)(2,1)} %get-tuple-element.10.v_ref), custom_call_target="tpu_custom_call" | custom-call | tf_op jit(solution)/shard_map/high/pallas_call | solution.py:223
  186.3 31.1 %home.1.g_ref = bf16[8,16,2,32,128]{4,3,2,1,0:T(8,128)(2,1)} custom-call(bf16[8,16,2,32,128]{4,3,2,1,0:T(8,128)(2,1)} %high.1.f), custom_call_target="tpu_custom_call" | custom-call | tf_op jit(solution)/shard_map/home/pallas_call | solution.py:254
  217.3 12.3 %last.1 = f32[8,16,8,2048]{3,2,1,0:T(8,128)} custom-call(bf16[8,16,2,32,128]{4,3,2,1,0:T(8,128)(2,1)} %home.1.g_ref, bf16[2,32,2048]{2,1,0:T(8,128)(2,1)} %bitcast.16), custom_call_target="tpu_custom_call" | custom-call | tf_op jit(solution)/shard_map/last/pallas_call | solution.py:279
  (1 shorter events, 0.0 us)

commit v2 on v0

v2 whole, which is shorter than its diff:
```python
import jax
import jax.numpy as jnp
from jax import lax
from jax.experimental import pallas as pl
from jax.experimental.pallas import tpu as pltpu
from jax.sharding import PartitionSpec as P

MESH = pl.DeviceIdType.MESH
F32, BF16 = jnp.float32, jnp.bfloat16
ANY = pl.BlockSpec(memory_space=pl.ANY)
LIMIT = 56 * 2**20


def place():
    return lax.axis_index("gx"), lax.axis_index("gy")


CHUNKS = 8
PAIR = 2


def target(gy, beta):
    c, y0, zh = gy & 1, (gy >> 1) & 1, gy >> 3
    return ((zh ^ beta) << 2) | (c << 1) | (y0 ^ beta)


def origin(gx, beta, half):
    return (((gx >> 2) ^ beta) << 3) | (half << 2) | (((gx & 1) ^ beta) << 1) | ((gx >> 1) & 1)


def boxes(k):
    return pl.ds(k * PAIR, PAIR)


def remote(src, dst, send, recv, device):
    return pltpu.make_async_remote_copy(
        src_ref=src, dst_ref=dst, send_sem=send, recv_sem=recv,
        device_id=device, device_id_type=MESH)


def drain(ref, sem):
    pltpu.make_async_copy(ref, ref, sem).wait()


def main_kernel(samples, interp, translation, g_ref,
                x, raw, w, v, o, t, f, low_state, low_turned, high_state, high_turned,
                x_recv, w_recv, v_recv, t_recv, sent, here):
    gx, gy = place()
    half = (gy >> 2) & 1
    far, core, mate = gy ^ 8, gy ^ 1, gx ^ 4
    x_sent, w_sent, v_sent, o_sent, f_sent, g_recv = [sent.at[i] for i in range(6)]
    own_target = [target(gy, beta) == gx for beta in range(2)]

    load = [pltpu.make_async_copy(translation, raw, here.at[0]),
            pltpu.make_async_copy(interp.at[0], w.at[gy, :, 0], here.at[1]),
            pltpu.make_async_copy(interp.at[1], w.at[gy, :, 1], here.at[2])]
    for copy in load:
        copy.start()

    barrier = pltpu.get_barrier_semaphore()

    def hello(device):
        pl.semaphore_signal(barrier, inc=1, device_id=device, device_id_type=MESH)

    for m in (1, 2, 4, 6, 8):
        hello((gx, gy ^ m))
    for m in range(1, 8):
        hello((gx ^ m, gy))
    for beta in range(2):
        for side in range(2):
            source = origin(gx, beta, side)
            for m in range(1, 8):
                hello((gx ^ m, source))

            @pl.when(source != gy)
            def _():
                hello((gx, source))
    selves = jnp.where(own_target[0], 1, 0) + jnp.where(own_target[1], 1, 0)
    pl.semaphore_wait(barrier, 12 + 32 - selves)

    def send_samples(k, carry):
        for m in range(1, 8):
            remote(samples.at[gx ^ m, :, boxes(k)], x.at[k, gx], x_sent, x_recv.at[k],
                   (gx ^ m, gy)).start()
        pltpu.make_async_copy(samples.at[gx, :, boxes(k)], x.at[k, gx], x_recv.at[k]).start()
        return carry

    lax.fori_loop(0, CHUNKS, send_samples, 0)

    for copy in load:
        copy.wait()

    def pack(b, carry):
        for level in range(7):
            pair = jnp.concatenate([raw[level, 0, b], raw[level, 1, b]], axis=1)
            if level < 4:
                w[gy, b, 2 + level] = pair
            else:
                v[gx, b, level - 4] = pair
        return carry

    lax.fori_loop(0, 16, pack, 0)

    def send_w(slot, k, flip, kind):
        remote(w.at[slot, boxes(k)], w.at[slot, boxes(k)], w_sent, w_recv.at[kind, k],
               (gx, gy ^ flip)).start()

    def got_w(k, kind):
        drain(w.at[0, boxes(k)], w_recv.at[kind, k])

    def own_w(k):
        send_w(gy, k, 8, 0)
        for i, m in enumerate((2, 4, 6)):
            send_w(gy, k, m, 1 + i)
        send_w(gy, k, 1, 7)

    def far_w(k):
        got_w(k, 0)
        for i, m in enumerate((2, 4, 6)):
            send_w(far, k, m, 4 + i)
        send_w(far, k, 1, 7)

    def core_w(k):
        for i, m in enumerate((2, 4, 6)):
            got_w(k, 1 + i)
            send_w(gy ^ m, k, 1, 7)
        for i, m in enumerate((2, 4, 6)):
            got_w(k, 4 + i)
            send_w(far ^ m, k, 1, 7)

    def send_v(slot, k, flip, kind):
        remote(v.at[slot, boxes(k)], v.at[slot, boxes(k)], v_sent, v_recv.at[kind, k],
               (gx ^ flip, gy)).start()

    def own_v(k):
        send_v(gx, k, 4, 0)
        for m in (1, 2, 3):
            send_v(gx, k, m, 1)

    def mate_v(k):
        drain(v.at[0, boxes(k)], v_recv.at[0, k])
        for m in (1, 2, 3):
            send_v(mate, k, m, 1)

    first = lax.broadcasted_iota(jnp.int32, (32, 128), 1) < 64

    def low(k):
        def one(beta, carry):
            b = k * PAIR + beta
            for g in range(16):
                rows = x[k, :, g, beta].reshape(64, 128)
                table = w[g, b, 0:2].reshape(64, 128)
                got = lax.dot_general(
                    table, rows, (((1,), (1,)), ((), ())), preferred_element_type=F32)
                pair = jnp.concatenate([got[:32], got[32:]], axis=1)
                low_state[0, g] = pair.astype(BF16)
                low_turned[0, g] = turn(pair, first)
            for level in range(4):
                now, later = level % 2, (level + 1) % 2
                for g in range(16):
                    h = g ^ (1 << level)
                    right = jnp.concatenate(
                        [low_state[now, g], low_state[now, h],
                         low_turned[now, g], low_turned[now, h]], axis=0)
                    got = jnp.dot(w[g, b, 2 + level], right, preferred_element_type=F32)
                    if level == 3:
                        o[g, b] = got.astype(BF16)
                    else:
                        low_state[later, g] = got.astype(BF16)
                        low_turned[later, g] = turn(got, first)
            return carry

        lax.fori_loop(0, PAIR, one, 0)

    def send_o(k):
        def each(i, carry):
            gy2 = gy ^ i ^ ((gx & 3) << 1) ^ ((gx >> 2) << 3)
            for beta in range(2):
                gx2 = target(gy, beta)
                src = o.at[gy2, k * PAIR + beta]
                dst = t.at[k, gx, half, beta]
                mine = (gx2 == gx) & (gy2 == gy)

                @pl.when(mine)
                def _():
                    pltpu.make_async_copy(src, dst, t_recv.at[k]).start()

                @pl.when(jnp.logical_not(mine))
                def _():
                    remote(src, dst, o_sent, t_recv.at[k], (gx2, gy2)).start()
            return carry

        lax.fori_loop(0, 16, each, 0)

    def high(k):
        def one(beta, carry):
            b = k * PAIR + beta
            for g in range(8):
                for side in range(2):
                    tile = t[k, g, side, beta]
                    high_state[0, g, :, side * 128:side * 128 + 128] = tile
                    high_turned[0, g, :, side * 128:side * 128 + 128] = turn(
                        tile.astype(F32), first)
            for level in range(3):
                now, later = level % 2, (level + 1) % 2
                for g in range(8):
                    h = g ^ (1 << level)
                    right = jnp.concatenate(
                        [high_state[now, g], high_state[now, h],
                         high_turned[now, g], high_turned[now, h]], axis=0)
                    got = jnp.dot(v[g, b, level], right, preferred_element_type=F32)
                    left, rest = got[:, :128], got[:, 128:]
                    if level == 2:
                        f[g, b, 0] = jnp.where(first, left, pltpu.roll(rest, 64, 1)).astype(BF16)
                        f[g, b, 1] = jnp.where(first, pltpu.roll(left, 64, 1), rest).astype(BF16)
                    else:
                        high_state[later, g] = got.astype(BF16)
                        high_turned[later, g, :, :128] = turn(left, first)
                        high_turned[later, g, :, 128:] = turn(rest, first)
            return carry

        lax.fori_loop(0, PAIR, one, 0)

    def send_f(k):
        for m in range(1, 8):
            remote(f.at[gx ^ m, boxes(k)], g_ref.at[gx, boxes(k)], f_sent, g_recv,
                   (gx ^ m, gy)).start()
        pltpu.make_async_copy(f.at[gx, boxes(k)], g_ref.at[gx, boxes(k)], g_recv).start()

    for k in range(3):
        own_w(k)
    far_w(0)
    far_w(1)
    core_w(0)
    own_v(0)

    def step(k, carry):
        @pl.when(k < CHUNKS - 3)
        def _():
            own_w(k + 3)

        @pl.when(k < CHUNKS - 1)
        def _():
            own_v(k + 1)

        @pl.when(k < CHUNKS - 2)
        def _():
            far_w(k + 2)

        @pl.when(k < CHUNKS - 1)
        def _():
            core_w(k + 1)

        @pl.when(k < CHUNKS)
        def _():
            mate_v(k)
            drain(w.at[pl.ds(0, 8), boxes(k)], w_recv.at[7, k])
            drain(x.at[k], x_recv.at[k])
            low(k)
            send_o(k)

        @pl.when(k > 0)
        def _():
            drain(v.at[pl.ds(0, 6), boxes(k - 1)], v_recv.at[1, k - 1])
            drain(t.at[k - 1], t_recv.at[k - 1])
            high(k - 1)
            send_f(k - 1)

        return carry

    lax.fori_loop(0, CHUNKS + 1, step, 0)
    drain(g_ref, g_recv)
    drain(f.at[pl.ds(0, 7)], f_sent)
    drain(x.at[:, pl.ds(0, 7)], x_sent)
    drain(w.at[pl.ds(0, 15)], w_sent)
    drain(v.at[pl.ds(0, 7)], v_sent)
    for beta in range(2):
        @pl.when(own_target[beta])
        def _():
            drain(o.at[pl.ds(0, 15), pl.ds(0, 8)], o_sent)

        @pl.when(jnp.logical_not(own_target[beta]))
        def _():
            drain(o.at[:, pl.ds(0, 8)], o_sent)


def main(samples, interp, translation):
    dma = pltpu.SemaphoreType.DMA
    return pl.pallas_call(
        main_kernel,
        out_shape=jax.ShapeDtypeStruct((8, 16, 2, 32, 128), BF16),
        in_specs=[ANY] * 3,
        out_specs=ANY,
        scratch_shapes=[
            pltpu.VMEM((CHUNKS, 8, 16, PAIR, 8, 128), BF16),
            pltpu.VMEM((7, 2, 16, 32, 64), BF16),
            pltpu.VMEM((16, 16, 6, 32, 128), BF16),
            pltpu.VMEM((8, 16, 3, 32, 128), BF16),
            pltpu.VMEM((16, 16, 32, 128), BF16),
            pltpu.VMEM((CHUNKS, 8, 2, PAIR, 32, 128), BF16),
            pltpu.VMEM((8, 16, 2, 32, 128), BF16),
            pltpu.VMEM((2, 16, 32, 128), BF16),
            pltpu.VMEM((2, 16, 32, 128), BF16),
            pltpu.VMEM((2, 8, 32, 256), BF16),
            pltpu.VMEM((2, 8, 32, 256), BF16),
            dma((CHUNKS,)), dma((8, CHUNKS)), dma((2, CHUNKS)), dma((CHUNKS,)), dma((6,)), dma((3,)),
        ],
        compiler_params=pltpu.CompilerParams(
            collective_id=1, has_side_effects=True, vmem_limit_bytes=LIMIT),
        cost_estimate=pl.CostEstimate(
            flops=2 * 2**30, bytes_accessed=10 * 2**20, transcendentals=0),
        name="levels",
    )(samples, interp, translation)


def turn(pair, first):
    moved = pltpu.roll(pair, 64, 1)
    return jnp.where(first, -moved, moved).astype(BF16)


def last_kernel(g_ref, e_ref, r_ref):
    beta = pl.program_id(0) % 2
    table = jnp.concatenate([e_ref[0], -e_ref[1]], axis=0)
    for s in range(8):
        left = g_ref[s, 0].reshape(64, 128)
        got = lax.dot_general(
            left, table, (((0,), (0,)), ((), ())), preferred_element_type=F32)
        got = got.reshape(2, 8, 8, 128)
        for half in range(2):
            r_ref[:, origin(s, beta, half)] = got[half]


def last(g, e):
    return pl.pallas_call(
        last_kernel,
        grid=(16,),
        out_shape=jax.ShapeDtypeStruct((8, 16, 8, 2048), F32),
        in_specs=[pl.BlockSpec((8, 1, 2, 32, 128), lambda b: (0, b, 0, 0, 0)),
                  pl.BlockSpec((2, 32, 128), lambda b: (0, 0, b))],
        out_specs=pl.BlockSpec((8, 16, 8, 128), lambda b: (0, 0, 0, b)),
        compiler_params=pltpu.CompilerParams(vmem_limit_bytes=LIMIT),
        name="last",
    )(g, e)


def on_device(samples, interp, translation, evaluate):
    by_box = samples.reshape(8, 2048, 128).transpose(1, 0, 2).reshape(8, 16, 16, 8, 128)
    state = main(by_box, interp, translation)
    return last(state, evaluate.transpose(0, 2, 1)).reshape(1024, 2048)


def solution(mesh):
    in_specs = (
        P(("gx", "gy"), None),
        P(None, ("gx", "gy"), None, None),
        P(None, None, ("gx", "gy"), None, None),
        P(None, ("gx", "gy"), None),
    )
    out_specs = P(None, ("gx", "gy"))
    return jax.shard_map(
        on_device, mesh=mesh, in_specs=in_specs, out_specs=out_specs, check_vma=False
    )
```

time: 399 us -> 174 us (0.44)
  waiting for transfers between devices: 277 us -> 0 us
  Pallas kernels: 0 us -> 173 us
  blocking collectives: 68 us -> 0 us
  matrix products: 31.9 us -> 0 us
  local copies, waits for them, and re-layouts: 12.6 us -> 0 us
  other arithmetic: 4.05 us -> 0 us
    ppermute x7 -> x0, waiting for transfers between devices: 277 us -> none  [partner_2(): return lax.ppermute(block, axis, route)]
    pallas_call x0 -> x2, Pallas kernels: none -> 173 us  [the longest x1 161 us: main(): pl.pallas_call(main_kernel, out_shape=jax.ShapeDtypeStruct((8, 16, 2, 32,...]
    all_to_all x1 -> x0, blocking collectives: 68 us -> none  [on_device(): lax.all_to_all(samples, ('gx', 'gy'), split_axis=1, concat_axis=0, tiled=...]
    dot_general x29 -> x0, matrix products: 31.9 us -> none  [the longest x26 13.2 us: box_product(): jnp.einsum('bkj,bjr->bkr', weight, values, preferred_element_type=jnp.flo...]
    reshape x1 -> x0, local copies, waits for them, and re-layouts: 9.17 us -> none  [on_device(): return result.reshape(records, evaluate.shape[1])]
  transfers between devices with their start and end apart: 7 -> 0, of which waited for: 7 -> 0; matrix products, arithmetic and copies ran while one was open for 0% -> 0% of each run, Pallas kernels for 0% -> 0%
where the time goes in v2:
time: 174 us; the launch traced here: 173 us
  Pallas kernels  173 us (99%)
    pallas_call x1, Pallas kernels, main(): pl.pallas_call(main_kernel, out_shape=jax.ShapeDtypeStruct((8, 16, 2, 32,...  161 us
    pallas_call x1, Pallas kernels, last(): pl.pallas_call(last_kernel, grid=(16,), out_shape=jax.ShapeDtypeStruct((8...  12.3 us

profile of v2, /device:TPU:1, one launch (start us, length us, event | category | flops | bytes accessed | tf_op | source)
XLA Modules:
  0.0 173.3 jit_solution(17215231327292487143)
XLA Ops:
  0.0 161.0 %levels.1.g_ref = bf16[8,16,2,32,128]{4,3,2,1,0:T(8,128)(2,1)} custom-call(bf16[8,16,16,8,128]{4,3,2,1,0:T(8,128)(2,1)} %bitcast.7, bf16[2,16,32,128]{3,2,1,0:T(8,128)(2,1)} %interp.1, bf16[7,2,16,32,64]{4,3,2,1,0:T(8,128)(2,1)} %translation.1), custom_call_target="tpu_custom_call" | custom-call | flops 2147483648 | bytes 10485760 | tf_op jit(solution)/shard_map/levels/pallas_call | solution.py:289
  161.0 12.3 %last.1 = f32[8,16,8,2048]{3,2,1,0:T(8,128)} custom-call(bf16[8,16,2,32,128]{4,3,2,1,0:T(8,128)(2,1)} %levels.1.g_ref, bf16[2,32,2048]{2,1,0:T(8,128)(2,1)} %bitcast.8), custom_call_target="tpu_custom_call" | custom-call | tf_op jit(solution)/shard_map/last/pallas_call | solution.py:334

commit v3 on v2

--- a/solution.py
+++ b/solution.py
@@ -90,9 +90,15 @@
     for copy in load:
         copy.wait()
 
+    low_half = lax.broadcasted_iota(jnp.int32, (32, 128), 1) % 64 < 32
+
     def pack(b, carry):
         for level in range(7):
             pair = jnp.concatenate([raw[level, 0, b], raw[level, 1, b]], axis=1)
+            bit = (gy >> level) & 1 if level < 4 else (gx >> (level - 4)) & 1
+            wide = pair.astype(F32)
+            other = jnp.where(low_half, pltpu.roll(wide, 96, 1), pltpu.roll(wide, 32, 1))
+            pair = jnp.where(bit == 1, other, wide).astype(BF16)
             if level < 4:
                 w[gy, b, 2 + level] = pair
             else:
@@ -145,7 +151,7 @@
     first = lax.broadcasted_iota(jnp.int32, (32, 128), 1) < 64
 
     def low(k):
-        def one(beta, carry):
+        def box_of(beta, carry):
             b = k * PAIR + beta
             for g in range(16):
                 rows = x[k, :, g, beta].reshape(64, 128)
@@ -159,18 +165,22 @@
                 now, later = level % 2, (level + 1) % 2
                 for g in range(16):
                     h = g ^ (1 << level)
+                    if h < g:
+                        continue
                     right = jnp.concatenate(
                         [low_state[now, g], low_state[now, h],
                          low_turned[now, g], low_turned[now, h]], axis=0)
-                    got = jnp.dot(w[g, b, 2 + level], right, preferred_element_type=F32)
-                    if level == 3:
-                        o[g, b] = got.astype(BF16)
-                    else:
-                        low_state[later, g] = got.astype(BF16)
-                        low_turned[later, g] = turn(got, first)
+                    left = jnp.concatenate([w[g, b, 2 + level], w[h, b, 2 + level]], axis=0)
+                    both = jnp.dot(left, right, preferred_element_type=F32)
+                    for box, got in ((g, both[:32]), (h, both[32:])):
+                        if level == 3:
+                            o[box, b] = got.astype(BF16)
+                        else:
+                            low_state[later, box] = got.astype(BF16)
+                            low_turned[later, box] = turn(got, first)
             return carry
 
-        lax.fori_loop(0, PAIR, one, 0)
+        lax.fori_loop(0, PAIR, box_of, 0)
 
     def send_o(k):
         def each(i, carry):
@@ -193,7 +203,7 @@
         lax.fori_loop(0, 16, each, 0)
 
     def high(k):
-        def one(beta, carry):
+        def box_of(beta, carry):
             b = k * PAIR + beta
             for g in range(8):
                 for side in range(2):
@@ -205,21 +215,27 @@
                 now, later = level % 2, (level + 1) % 2
                 for g in range(8):
                     h = g ^ (1 << level)
+                    if h < g:
+                        continue
                     right = jnp.concatenate(
                         [high_state[now, g], high_state[now, h],
                          high_turned[now, g], high_turned[now, h]], axis=0)
-                    got = jnp.dot(v[g, b, level], right, preferred_element_type=F32)
-                    left, rest = got[:, :128], got[:, 128:]
-                    if level == 2:
-                        f[g, b, 0] = jnp.where(first, left, pltpu.roll(rest, 64, 1)).astype(BF16)
-                        f[g, b, 1] = jnp.where(first, pltpu.roll(left, 64, 1), rest).astype(BF16)
-                    else:
-                        high_state[later, g] = got.astype(BF16)
-                        high_turned[later, g, :, :128] = turn(left, first)
-                        high_turned[later, g, :, 128:] = turn(rest, first)
+                    left = jnp.concatenate([v[g, b, level], v[h, b, level]], axis=0)
+                    both = jnp.dot(left, right, preferred_element_type=F32)
+                    for box, got in ((g, both[:32]), (h, both[32:])):
+                        one, two = got[:, :128], got[:, 128:]
+                        if level == 2:
+                            f[box, b, 0] = jnp.where(
+                                first, one, pltpu.roll(two, 64, 1)).astype(BF16)
+                            f[box, b, 1] = jnp.where(
+                                first, pltpu.roll(one, 64, 1), two).astype(BF16)
+                        else:
+                            high_state[later, box] = got.astype(BF16)
+                            high_turned[later, box, :, :128] = turn(one, first)
+                            high_turned[later, box, :, 128:] = turn(two, first)
             return carry
 
-        lax.fori_loop(0, PAIR, one, 0)
+        lax.fori_loop(0, PAIR, box_of, 0)
 
     def send_f(k):
         for m in range(1, 8):
@@ -227,37 +243,36 @@
                    (gx ^ m, gy)).start()
         pltpu.make_async_copy(f.at[gx, boxes(k)], g_ref.at[gx, boxes(k)], g_recv).start()
 
-    for k in range(3):
-        own_w(k)
-    far_w(0)
-    far_w(1)
-    core_w(0)
-    own_v(0)
+    def upto(n, fn):
+        lax.fori_loop(0, n, lambda k, c: (fn(k), c)[1], 0)
+
+    upto(8, own_w)
+    upto(8, own_v)
+    upto(4, far_w)
+    upto(2, core_w)
+    upto(1, mate_v)
+
+    def ahead(k, by, fn):
+        @pl.when(k + by < CHUNKS)
+        def _():
+            fn(k + by)
+
+    def relays(k):
+        ahead(k, 4, far_w)
+        ahead(k, 2, core_w)
+        ahead(k, 1, mate_v)
 
     def step(k, carry):
-        @pl.when(k < CHUNKS - 3)
-        def _():
-            own_w(k + 3)
-
-        @pl.when(k < CHUNKS - 1)
-        def _():
-            own_v(k + 1)
-
-        @pl.when(k < CHUNKS - 2)
-        def _():
-            far_w(k + 2)
-
-        @pl.when(k < CHUNKS - 1)
-        def _():
-            core_w(k + 1)
+        pass
 
         @pl.when(k < CHUNKS)
         def _():
-            mate_v(k)
             drain(w.at[pl.ds(0, 8), boxes(k)], w_recv.at[7, k])
             drain(x.at[k], x_recv.at[k])
             low(k)
             send_o(k)
+
+        relays(k)
 
         @pl.when(k > 0)
         def _():
@@ -319,25 +334,30 @@
 
 
 def last_kernel(g_ref, e_ref, r_ref):
-    beta = pl.program_id(0) % 2
     table = jnp.concatenate([e_ref[0], -e_ref[1]], axis=0)
+    none = jnp.zeros((64, 128), BF16)
+    table = jnp.concatenate(
+        [jnp.concatenate([table[:, :128], none], axis=1),
+         jnp.concatenate([none, table[:, 128:]], axis=1)], axis=0)
     for s in range(8):
-        left = g_ref[s, 0].reshape(64, 128)
+        left = g_ref[s].reshape(128, 128)
         got = lax.dot_general(
             left, table, (((0,), (0,)), ((), ())), preferred_element_type=F32)
-        got = got.reshape(2, 8, 8, 128)
-        for half in range(2):
-            r_ref[:, origin(s, beta, half)] = got[half]
+        got = got.reshape(2, 8, 8, 256)
+        for beta in range(PAIR):
+            lanes = slice(beta * 128, beta * 128 + 128)
+            for half in range(2):
+                r_ref[:, origin(s, beta, half), :, lanes] = got[half, :, :, lanes]
 
 
 def last(g, e):
     return pl.pallas_call(
         last_kernel,
-        grid=(16,),
+        grid=(CHUNKS,),
         out_shape=jax.ShapeDtypeStruct((8, 16, 8, 2048), F32),
-        in_specs=[pl.BlockSpec((8, 1, 2, 32, 128), lambda b: (0, b, 0, 0, 0)),
-                  pl.BlockSpec((2, 32, 128), lambda b: (0, 0, b))],
-        out_specs=pl.BlockSpec((8, 16, 8, 128), lambda b: (0, 0, 0, b)),
+        in_specs=[pl.BlockSpec((8, PAIR, 2, 32, 128), lambda k: (0, k, 0, 0, 0)),
+                  pl.BlockSpec((2, 32, 256), lambda k: (0, 0, k))],
+        out_specs=pl.BlockSpec((8, 16, 8, 256), lambda k: (0, 0, 0, k)),
         compiler_params=pltpu.CompilerParams(vmem_limit_bytes=LIMIT),
         name="last",
     )(g, e)

time: 174 us -> 152 us (0.87)
  Pallas kernels: 173 us -> 151 us
    pallas_call x1, Pallas kernels: 161 us -> 143 us  [main(): pl.pallas_call(main_kernel, out_shape=jax.ShapeDtypeStruct((8, 16, 2, 32,...]
    pallas_call x1, Pallas kernels: 12.3 us -> 7.71 us  [last(): pl.pallas_call(last_kernel, grid=(CHUNKS,), out_shape=jax.ShapeDtypeStruc...]
where the time goes in v3:
time: 152 us; the launch traced here: 151 us
  Pallas kernels  151 us (99%)
    pallas_call x1, Pallas kernels, main(): pl.pallas_call(main_kernel, out_shape=jax.ShapeDtypeStruct((8, 16, 2, 32,...  143 us
    pallas_call x1, Pallas kernels, last(): pl.pallas_call(last_kernel, grid=(CHUNKS,), out_shape=jax.ShapeDtypeStruc...  7.71 us

profile of v3, /device:TPU:1, one launch (start us, length us, event | category | flops | bytes accessed | tf_op | source)
XLA Modules:
  0.0 151.0 jit_solution(5124331528812462517)
XLA Ops:
  0.0 143.2 %levels.1.g_ref = bf16[8,16,2,32,128]{4,3,2,1,0:T(8,128)(2,1)} custom-call(bf16[8,16,16,8,128]{4,3,2,1,0:T(8,128)(2,1)} %bitcast.7, bf16[2,16,32,128]{3,2,1,0:T(8,128)(2,1)} %interp.1, bf16[7,2,16,32,64]{4,3,2,1,0:T(8,128)(2,1)} %translation.1), custom_call_target="tpu_custom_call" | custom-call | flops 2147483648 | bytes 10485760 | tf_op jit(solution)/shard_map/levels/pallas_call | solution.py:304
  143.2 7.7 %last.1 = f32[8,16,8,2048]{3,2,1,0:T(8,128)} custom-call(bf16[8,16,2,32,128]{4,3,2,1,0:T(8,128)(2,1)} %levels.1.g_ref, bf16[2,32,2048]{2,1,0:T(8,128)(2,1)} %bitcast.8), custom_call_target="tpu_custom_call" | custom-call | tf_op jit(solution)/shard_map/last/pallas_call | solution.py:354

commit v4 on v3

--- a/solution.py
+++ b/solution.py
@@ -47,6 +47,8 @@
                 x_recv, w_recv, v_recv, t_recv, sent, here):
     gx, gy = place()
     half = (gy >> 2) & 1
+    x_up = (gx & 4) | ((gx + 1) & 3)
+    x_down = (gx & 4) | ((gx + 3) & 3)
     far, core, mate = gy ^ 8, gy ^ 1, gx ^ 4
     x_sent, w_sent, v_sent, o_sent, f_sent, g_recv = [sent.at[i] for i in range(6)]
     own_target = [target(gy, beta) == gx for beta in range(2)]
@@ -85,7 +87,7 @@
         pltpu.make_async_copy(samples.at[gx, :, boxes(k)], x.at[k, gx], x_recv.at[k]).start()
         return carry
 
-    lax.fori_loop(0, CHUNKS, send_samples, 0)
+    lax.fori_loop(0, 2, send_samples, 0)
 
     for copy in load:
         copy.wait()
@@ -134,19 +136,33 @@
             got_w(k, 4 + i)
             send_w(far ^ m, k, 1, 7)
 
-    def send_v(slot, k, flip, kind):
-        remote(v.at[slot, boxes(k)], v.at[slot, boxes(k)], v_sent, v_recv.at[kind, k],
-               (gx ^ flip, gy)).start()
-
-    def own_v(k):
-        send_v(gx, k, 4, 0)
-        for m in (1, 2, 3):
-            send_v(gx, k, m, 1)
-
-    def mate_v(k):
-        drain(v.at[0, boxes(k)], v_recv.at[0, k])
-        for m in (1, 2, 3):
-            send_v(mate, k, m, 1)
+    def send_v(slot, j, part, to, kind):
+        rows = (pl.ds(j * 4, 2), pl.ds(j * 4 + 2, 2), pl.ds(j * 4, 4))[part]
+        remote(v.at[slot, rows], v.at[slot, rows], v_sent, v_recv.at[kind, j], (to, gy)).start()
+
+    def got_v(j, kind):
+        drain(v.at[0, pl.ds(j * 4, 4)], v_recv.at[kind, j])
+
+    def own_v(j):
+        send_v(gx, j, 2, mate, 0)
+        send_v(gx, j, 2, x_up, 1)
+        send_v(gx, j, 2, x_down, 2)
+
+    def mate_v(j):
+        got_v(j, 0)
+        send_v(mate, j, 2, x_up, 3)
+        send_v(mate, j, 2, x_down, 4)
+
+    def relay_v(j, flip, kind):
+        got_v(j, kind)
+        send_v(x_down ^ flip, j, 0, x_up, 5)
+        got_v(j, kind + 1)
+        send_v(x_up ^ flip, j, 1, x_down, 5)
+
+    def drain_v(k):
+        @pl.when(k % 2 == 0)
+        def _():
+            drain(v.at[pl.ds(0, 2), pl.ds((k // 2) * 4, 4)], v_recv.at[5, k // 2])
 
     first = lax.broadcasted_iota(jnp.int32, (32, 128), 1) < 64
 
@@ -247,10 +263,10 @@
         lax.fori_loop(0, n, lambda k, c: (fn(k), c)[1], 0)
 
     upto(8, own_w)
-    upto(8, own_v)
+    upto(4, own_v)
+    lax.fori_loop(2, CHUNKS, send_samples, 0)
     upto(4, far_w)
     upto(2, core_w)
-    upto(1, mate_v)
 
     def ahead(k, by, fn):
         @pl.when(k + by < CHUNKS)
@@ -260,7 +276,15 @@
     def relays(k):
         ahead(k, 4, far_w)
         ahead(k, 2, core_w)
-        ahead(k, 1, mate_v)
+
+        @pl.when(k < 4)
+        def _():
+            relay_v(k, 0, 1)
+            mate_v(k)
+
+        @pl.when((k > 0) & (k < 5))
+        def _():
+            relay_v(k - 1, 4, 3)
 
     def step(k, carry):
         pass
@@ -274,16 +298,16 @@
 
         relays(k)
 
-        @pl.when(k > 0)
-        def _():
-            drain(v.at[pl.ds(0, 6), boxes(k - 1)], v_recv.at[1, k - 1])
-            drain(t.at[k - 1], t_recv.at[k - 1])
-            high(k - 1)
-            send_f(k - 1)
+        @pl.when(k >= 3)
+        def _():
+            drain_v(k - 3)
+            drain(t.at[k - 3], t_recv.at[k - 3])
+            high(k - 3)
+            send_f(k - 3)
 
         return carry
 
-    lax.fori_loop(0, CHUNKS + 1, step, 0)
+    lax.fori_loop(0, CHUNKS + 3, step, 0)
     drain(g_ref, g_recv)
     drain(f.at[pl.ds(0, 7)], f_sent)
     drain(x.at[:, pl.ds(0, 7)], x_sent)
@@ -318,7 +342,7 @@
             pltpu.VMEM((2, 16, 32, 128), BF16),
             pltpu.VMEM((2, 8, 32, 256), BF16),
             pltpu.VMEM((2, 8, 32, 256), BF16),
-            dma((CHUNKS,)), dma((8, CHUNKS)), dma((2, CHUNKS)), dma((CHUNKS,)), dma((6,)), dma((3,)),
+            dma((CHUNKS,)), dma((8, CHUNKS)), dma((6, 4)), dma((CHUNKS,)), dma((6,)), dma((3,)),
         ],
         compiler_params=pltpu.CompilerParams(
             collective_id=1, has_side_effects=True, vmem_limit_bytes=LIMIT),
@@ -333,31 +357,49 @@
     return jnp.where(first, -moved, moved).astype(BF16)
 
 
-def last_kernel(g_ref, e_ref, r_ref):
+def last_kernel(g_ref, e_ref, r_ref, g, r, load, store):
+    loads = [pltpu.make_async_copy(g_ref.at[:, boxes(k)], g.at[:, boxes(k)], load.at[k])
+             for k in range(CHUNKS)]
+    for copy in loads:
+        copy.start()
     table = jnp.concatenate([e_ref[0], -e_ref[1]], axis=0)
     none = jnp.zeros((64, 128), BF16)
-    table = jnp.concatenate(
-        [jnp.concatenate([table[:, :128], none], axis=1),
-         jnp.concatenate([none, table[:, 128:]], axis=1)], axis=0)
-    for s in range(8):
-        left = g_ref[s].reshape(128, 128)
-        got = lax.dot_general(
-            left, table, (((0,), (0,)), ((), ())), preferred_element_type=F32)
-        got = got.reshape(2, 8, 8, 256)
-        for beta in range(PAIR):
-            lanes = slice(beta * 128, beta * 128 + 128)
-            for half in range(2):
-                r_ref[:, origin(s, beta, half), :, lanes] = got[half, :, :, lanes]
+    stores = []
+    for k in range(CHUNKS):
+        at = k * 256
+        pair = jnp.concatenate(
+            [jnp.concatenate([table[:, at:at + 128], none], axis=1),
+             jnp.concatenate([none, table[:, at + 128:at + 256]], axis=1)], axis=0)
+        loads[k].wait()
+        for s in range(8):
+            left = g[s, k * PAIR:k * PAIR + PAIR].reshape(128, 128)
+            got = lax.dot_general(
+                left, pair, (((0,), (0,)), ((), ())), preferred_element_type=F32)
+            got = got.reshape(2, 8, 8, 256)
+            for beta in range(PAIR):
+                lanes = slice(beta * 128, beta * 128 + 128)
+                for half in range(2):
+                    r[:, origin(s, beta, half), :, at + lanes.start:at + lanes.stop] = (
+                        got[half, :, :, lanes])
+        if k % 2 == 1:
+            wide = pl.ds(at - 256, 512)
+            copy = pltpu.make_async_copy(
+                r.at[:, :, :, wide], r_ref.at[:, :, :, wide], store.at[k // 2])
+            copy.start()
+            stores.append(copy)
+    for copy in stores:
+        copy.wait()
 
 
 def last(g, e):
+    dma = pltpu.SemaphoreType.DMA
     return pl.pallas_call(
         last_kernel,
-        grid=(CHUNKS,),
         out_shape=jax.ShapeDtypeStruct((8, 16, 8, 2048), F32),
-        in_specs=[pl.BlockSpec((8, PAIR, 2, 32, 128), lambda k: (0, k, 0, 0, 0)),
-                  pl.BlockSpec((2, 32, 256), lambda k: (0, 0, k))],
-        out_specs=pl.BlockSpec((8, 16, 8, 256), lambda k: (0, 0, 0, k)),
+        in_specs=[ANY, pl.BlockSpec(memory_space=pltpu.VMEM)],
+        out_specs=ANY,
+        scratch_shapes=[pltpu.VMEM(g.shape, BF16), pltpu.VMEM((8, 16, 8, 2048), F32),
+                        dma((CHUNKS,)), dma((CHUNKS // 2,))],
         compiler_params=pltpu.CompilerParams(vmem_limit_bytes=LIMIT),
         name="last",
     )(g, e)

time: 152 us -> 142 us (0.934)
  Pallas kernels: 151 us -> 142 us
    pallas_call x1, Pallas kernels: 143 us -> 136 us  [main(): pl.pallas_call(main_kernel, out_shape=jax.ShapeDtypeStruct((8, 16, 2, 32,...]
    pallas_call x1, Pallas kernels: 7.71 us -> 5.98 us  [last(): pl.pallas_call(last_kernel, out_shape=jax.ShapeDtypeStruct((8, 16, 8, 204...]
where the time goes in v4:
time: 142 us
  Pallas kernels  142 us (100%)
    pallas_call x1, Pallas kernels, main(): pl.pallas_call(main_kernel, out_shape=jax.ShapeDtypeStruct((8, 16, 2, 32,...  136 us
    pallas_call x1, Pallas kernels, last(): pl.pallas_call(last_kernel, out_shape=jax.ShapeDtypeStruct((8, 16, 8, 204...  5.98 us

profile of v4, /device:TPU:1, one launch (start us, length us, event | category | flops | bytes accessed | tf_op | source)
XLA Modules:
  0.0 141.9 jit_solution(12414543718350818811)
XLA Ops:
  0.0 136.0 %levels.1.g_ref = bf16[8,16,2,32,128]{4,3,2,1,0:T(8,128)(2,1)} custom-call(bf16[8,16,16,8,128]{4,3,2,1,0:T(8,128)(2,1)} %bitcast.7, bf16[2,16,32,128]{3,2,1,0:T(8,128)(2,1)} %interp.1, bf16[7,2,16,32,64]{4,3,2,1,0:T(8,128)(2,1)} %translation.1), custom_call_target="tpu_custom_call" | custom-call | flops 2147483648 | bytes 10485760 | tf_op jit(solution)/shard_map/levels/pallas_call | solution.py:328
  136.0 6.0 %last.1 = f32[8,16,8,2048]{3,2,1,0:T(8,128)} custom-call(bf16[8,16,2,32,128]{4,3,2,1,0:T(8,128)(2,1)} %levels.1.g_ref, bf16[2,32,2048]{2,1,0:T(8,128)(2,1)} %bitcast.8), custom_call_target="tpu_custom_call" | custom-call | tf_op jit(solution)/shard_map/last/pallas_call | solution.py:396

commit v5 on v0

v5 whole, which is shorter than its diff:
```python
import jax
import jax.numpy as jnp
from jax import lax
from jax.experimental import pallas as pl
from jax.experimental.pallas import tpu as pltpu
from jax.sharding import PartitionSpec as P

MESH = pl.DeviceIdType.MESH
F32, BF16 = jnp.float32, jnp.bfloat16
ANY = pl.BlockSpec(memory_space=pl.ANY)
LIMIT = 56 * 2**20


def place():
    return lax.axis_index("gx"), lax.axis_index("gy")


PARTS = 4


def block_of(q, y):
    return ((q >> 1) << 3) | (y << 1) | (q & 1)


def z_of(q):
    return (q >> 1) ^ (q & 1)


def q_of(z, e):
    return z if e == 0 else 3 - z


def remote(src, dst, send, recv, device):
    return pltpu.make_async_remote_copy(
        src_ref=src, dst_ref=dst, send_sem=send, recv_sem=recv,
        device_id=device, device_id_type=MESH)


def drain(ref, sem):
    pltpu.make_async_copy(ref, ref, sem).wait()


def main_kernel(samples, interp, translation, g_ref,
                x, raw, own_w, own_v, w, v, o, t, f, low_state, low_turned, high_state, high_turned,
                x_recv, w_recv, t_recv, sent, here):
    gx, gy = place()
    across, zl = gx & 3, gx >> 2
    y, q = (gy >> 1) & 3, ((gy >> 3) << 1) | (gy & 1)
    x_sent, w_sent, pass_sent, v_sent, o_sent, f_sent, v_recv, g_recv = [sent.at[i] for i in range(8)]
    own_z = z_of(q) == zl

    load = [pltpu.make_async_copy(translation, raw, here.at[0]),
            pltpu.make_async_copy(interp.at[0], own_w.at[:, 0], here.at[1]),
            pltpu.make_async_copy(interp.at[1], own_w.at[:, 1], here.at[2])]
    for copy in load:
        copy.start()

    barrier = pltpu.get_barrier_semaphore()

    def hello(device):
        pl.semaphore_signal(barrier, inc=1, device_id=device, device_id_type=MESH)

    def hello_samples(i, carry):
        hello((gx ^ (i & 7), block_of(q ^ (i >> 3), y)))
        return carry

    lax.fori_loop(1, 32, hello_samples, 0)
    for m in (1, 2, 3):
        hello((gx, block_of(q, y ^ m)))
    for e in range(2):
        source_q = q_of(zl, e)

        def hello_state(i, carry):
            gx1, gy1 = i & 7, block_of(source_q, i >> 3)

            @pl.when((gx1 != gx) | (gy1 != gy))
            def _():
                hello((gx1, gy1))
            return carry

        lax.fori_loop(0, 32, hello_state, 0)

    for copy in load:
        copy.wait()
    low_half = lax.broadcasted_iota(jnp.int32, (32, 128), 1) % 64 < 32

    def pack(b, carry):
        for level in range(7):
            pair = jnp.concatenate([raw[level, 0, b], raw[level, 1, b]], axis=1)
            bit = (gy >> level) & 1 if level < 4 else (gx >> (level - 4)) & 1
            wide = pair.astype(F32)
            other = jnp.where(low_half, pltpu.roll(wide, 96, 1), pltpu.roll(wide, 32, 1))
            pair = jnp.where(bit == 1, other, wide).astype(BF16)
            if level < 4:
                own_w[b, 2 + level] = pair
            else:
                own_v[b, level - 4] = pair
        return carry

    lax.fori_loop(0, 16, pack, 0)
    pl.semaphore_wait(barrier, 31 + 3 + 64 - jnp.where(own_z, 1, 0))

    def send_samples(part, those=range(8)):
        to = block_of(q ^ part, y)
        for m in those:
            src = samples.at[gx ^ m, :, pl.ds((q ^ part) * 4, 4)]
            if m == 0 and part == 0:
                pltpu.make_async_copy(src, x.at[part, gx], x_recv.at[part]).start()
            else:
                remote(src, x.at[part, gx], x_sent, x_recv.at[part], (gx ^ m, to)).start()

    def own(i):
        beta = i ^ across
        for m in range(4):
            src, dst = own_w.at[(q ^ m) * 4 + beta], w.at[beta, y, q]
            if m == 0:
                pltpu.make_async_copy(src, dst, w_recv.at[0, i]).start()
            else:
                remote(src, dst, w_sent, w_recv.at[0, i], (gx, block_of(q ^ m, y))).start()

    def along_y(i):
        beta = i ^ across
        drain(w.at[beta, y], w_recv.at[0, i])
        for piece in range(4):
            mine = w.at[beta, y, piece]
            for m in (1, 3, 2):
                remote(mine, mine, pass_sent, w_recv.at[1, i], (gx, block_of(q, y ^ m))).start()

    def send_v():
        for m in range(8):
            gx2 = gx ^ m
            z2 = gx2 >> 2
            for e in range(2):
                q2 = z2 if e == 0 else 3 - z2
                src, dst = own_v.at[q2 * 4 + (gx2 & 3)], v.at[gx, e]
                if m == 0:
                    pltpu.make_async_copy(src, dst, v_recv).start()
                else:
                    remote(src, dst, v_sent, v_recv, (gx2, gy)).start()

    first = lax.broadcasted_iota(jnp.int32, (32, 128), 1) < 64

    def low(part, beta):
        for g in range(16):
            gq, g_y = ((g >> 3) << 1) | (g & 1), (g >> 1) & 3
            rows = x[part, :, g, beta].reshape(64, 128)
            table = w[beta, g_y, gq, 0:2].reshape(64, 128)
            got = lax.dot_general(
                table, rows, (((1,), (1,)), ((), ())), preferred_element_type=F32)
            pair = jnp.concatenate([got[:32], got[32:]], axis=1)
            low_state[0, g] = pair.astype(BF16)
            low_turned[0, g] = turn(pair, first)
        for level in range(4):
            now, later = level % 2, (level + 1) % 2
            for g in range(16):
                h = g ^ (1 << level)
                if h < g:
                    continue
                right = jnp.concatenate(
                    [low_state[now, g], low_state[now, h],
                     low_turned[now, g], low_turned[now, h]], axis=0)
                left = jnp.concatenate(
                    [w[beta, (i >> 1) & 3, ((i >> 3) << 1) | (i & 1), 2 + level] for i in (g, h)],
                    axis=0)
                both = jnp.dot(left, right, preferred_element_type=F32)
                for box, got in ((g, both[:32]), (h, both[32:])):
                    if level == 3:
                        o[part, beta, box] = got.astype(BF16)
                    else:
                        low_state[later, box] = got.astype(BF16)
                        low_turned[later, box] = turn(got, first)

    def send_o(part):
        spread = (across << 1) ^ (zl << 3)

        def each(i, carry):
            beta = (i & 3) ^ across
            gx2 = z_of(q) * 4 + beta
            gy2 = gy ^ (i >> 2) ^ ((i & 3) << 1) ^ spread
            src, dst = o.at[part, beta, gy2], t.at[part, gx, q >> 1, y]
            mine = (gx2 == gx) & (gy2 == gy)

            @pl.when(mine)
            def _():
                pltpu.make_async_copy(src, dst, t_recv.at[part]).start()

            @pl.when(jnp.logical_not(mine))
            def _():
                remote(src, dst, o_sent, t_recv.at[part], (gx2, gy2)).start()
            return carry

        lax.fori_loop(0, 64, each, 0)

    def high(part):
        def box_of(e, carry):
            for g in range(8):
                for side in range(4):
                    lanes = slice(side * 128, side * 128 + 128)
                    tile = t[part, g, e, side]
                    high_state[0, g, :, lanes] = tile
                    high_turned[0, g, :, lanes] = turn(tile.astype(F32), first)
            for level in range(3):
                now, later = level % 2, (level + 1) % 2
                for g in range(8):
                    h = g ^ (1 << level)
                    if h < g:
                        continue
                    right = jnp.concatenate(
                        [high_state[now, g], high_state[now, h],
                         high_turned[now, g], high_turned[now, h]], axis=0)
                    left = jnp.concatenate([v[g, e, level], v[h, e, level]], axis=0)
                    both = jnp.dot(left, right, preferred_element_type=F32)
                    for box, got in ((g, both[:32]), (h, both[32:])):
                        piece = [got[:, i * 128:i * 128 + 128] for i in range(4)]
                        if level == 2:
                            for two in range(2):
                                one, other = piece[2 * two], piece[2 * two + 1]
                                f[part, box, e, two, 0] = jnp.where(
                                    first, one, pltpu.roll(other, 64, 1)).astype(BF16)
                                f[part, box, e, two, 1] = jnp.where(
                                    first, pltpu.roll(one, 64, 1), other).astype(BF16)
                        else:
                            high_state[later, box] = got.astype(BF16)
                            for i in range(4):
                                high_turned[later, box, :, i * 128:i * 128 + 128] = turn(
                                    piece[i], first)
            return carry

        lax.fori_loop(0, 2, box_of, 0)

    def send_f(part):
        for m in range(1, 8):
            remote(f.at[part, gx ^ m], g_ref.at[gx, part], f_sent, g_recv, (gx ^ m, gy)).start()
        pltpu.make_async_copy(f.at[part, gx], g_ref.at[gx, part], g_recv).start()

    def low_part(part, weights):
        def each(i, carry):
            if weights:
                drain(w.at[pl.ds(0, 3), 0], w_recv.at[1, i])
            low(part, i ^ across)
            return carry

        drain(x.at[part], x_recv.at[part])
        lax.fori_loop(0, 4, each, 0)
        send_o(part)

    def high_part(part):
        drain(t.at[part], t_recv.at[part])
        high(part)
        send_f(part)

    own(0)
    own(1)
    own(2)
    own(3)
    send_samples(0, (0, 1, 2, 3))
    send_samples(1, (0, 1, 2, 3))
    along_y(0)
    send_samples(0, (4,))
    send_samples(2, (5,))
    send_samples(2, (2,))
    send_samples(0, (5,))
    send_samples(2, (4,))
    send_samples(2, (3,))
    along_y(1)
    send_samples(0, (6,))
    send_samples(2, (7,))
    send_samples(2, (0,))
    send_samples(0, (7,))
    send_samples(2, (6,))
    send_samples(2, (1,))
    along_y(2)
    send_samples(1, (4,))
    send_samples(3, (5,))
    send_samples(3, (2,))
    send_samples(1, (5,))
    send_samples(3, (4,))
    send_samples(3, (3,))
    along_y(3)
    send_samples(1, (6,))
    send_samples(3, (7,))
    send_samples(3, (0,))
    send_samples(1, (7,))
    send_samples(3, (6,))
    send_samples(3, (1,))
    send_v()
    for step in range(PARTS + 2):
        if step < PARTS:
            low_part(((0, 2, 1, 3))[step], step == 0)
        if step == 2:
            drain(v, v_recv)
        if step >= 2:
            high_part(((0, 2, 1, 3))[step - 2])
    drain(g_ref, g_recv)
    drain(f.at[:, pl.ds(0, 7)], f_sent)
    drain(x.at[pl.ds(0, 3)], x_sent)
    drain(x.at[3, pl.ds(0, 7)], x_sent)
    drain(own_w.at[pl.ds(0, 12)], w_sent)
    drain(w.at[pl.ds(0, 3)], pass_sent)
    drain(v.at[pl.ds(0, 7)], v_sent)
    drain(o.at[:, pl.ds(0, 3)], o_sent)

    @pl.when(own_z)
    def _():
        drain(o.at[:, 3, pl.ds(0, 15)], o_sent)

    @pl.when(jnp.logical_not(own_z))
    def _():
        drain(o.at[:, 3], o_sent)


def main(samples, interp, translation):
    dma = pltpu.SemaphoreType.DMA
    return pl.pallas_call(
        main_kernel,
        out_shape=jax.ShapeDtypeStruct((8, PARTS, 2, 2, 2, 32, 128), BF16),
        in_specs=[ANY] * 3,
        out_specs=ANY,
        scratch_shapes=[
            pltpu.VMEM((PARTS, 8, 16, 4, 8, 128), BF16),
            pltpu.VMEM((7, 2, 16, 32, 64), BF16),
            pltpu.VMEM((16, 6, 32, 128), BF16),
            pltpu.VMEM((16, 3, 32, 128), BF16),
            pltpu.VMEM((4, 4, 4, 6, 32, 128), BF16),
            pltpu.VMEM((8, 2, 3, 32, 128), BF16),
            pltpu.VMEM((PARTS, 4, 16, 32, 128), BF16),
            pltpu.VMEM((PARTS, 8, 2, 4, 32, 128), BF16),
            pltpu.VMEM((PARTS, 8, 2, 2, 2, 32, 128), BF16),
            pltpu.VMEM((2, 16, 32, 128), BF16),
            pltpu.VMEM((2, 16, 32, 128), BF16),
            pltpu.VMEM((2, 8, 32, 512), BF16),
            pltpu.VMEM((2, 8, 32, 512), BF16),
            dma((PARTS,)), dma((2, 4)), dma((PARTS,)), dma((8,)), dma((3,)),
        ],
        compiler_params=pltpu.CompilerParams(
            collective_id=1, has_side_effects=True, vmem_limit_bytes=LIMIT),
        cost_estimate=pl.CostEstimate(
            flops=2 * 2**30, bytes_accessed=10 * 2**20, transcendentals=0),
        name="levels",
    )(samples, interp, translation)


def turn(pair, first):
    moved = pltpu.roll(pair, 64, 1)
    return jnp.where(first, -moved, moved).astype(BF16)


def last_kernel(g_ref, e_ref, r_ref, g, r, load, store):
    places = [(z_of(k >> 1) * 4 + (k & 1) * 2, k >> 2) for k in range(8)]
    loads = [pltpu.make_async_copy(g_ref.at[pl.ds(a, 2), :, e], g.at[pl.ds(a, 2), :, e], load.at[k])
             for k, (a, e) in enumerate(places)]
    for copy in loads:
        copy.start()
    table = jnp.concatenate([e_ref[0], -e_ref[1]], axis=0)
    none = jnp.zeros((64, 128), BF16)
    stores = []
    for k, (a, e) in enumerate(places):
        at = k * 256
        pair = jnp.concatenate(
            [jnp.concatenate([table[:, at:at + 128], none], axis=1),
             jnp.concatenate([none, table[:, at + 128:at + 256]], axis=1)], axis=0)
        loads[k].wait()
        for part in range(PARTS):
            for two in range(2):
                left = jnp.concatenate(
                    [g[a + i, part, e, two].reshape(64, 128) for i in range(2)], axis=0)
                got = lax.dot_general(
                    left, pair, (((0,), (0,)), ((), ())), preferred_element_type=F32)
                got = got.reshape(2, 8, 8, 256)
                for side in range(2):
                    gy1 = block_of((k >> 1) ^ part, 2 * two + side)
                    r[:, gy1, :, at:at + 256] = got[side]
        if k % 2 == 1:
            wide = pl.ds(at - 256, 512)
            copy = pltpu.make_async_copy(
                r.at[:, :, :, wide], r_ref.at[:, :, :, wide], store.at[k // 2])
            copy.start()
            stores.append(copy)
    for copy in stores:
        copy.wait()


def last(g, e):
    dma = pltpu.SemaphoreType.DMA
    return pl.pallas_call(
        last_kernel,
        out_shape=jax.ShapeDtypeStruct((8, 16, 8, 2048), F32),
        in_specs=[ANY, pl.BlockSpec(memory_space=pltpu.VMEM)],
        out_specs=ANY,
        scratch_shapes=[pltpu.VMEM(g.shape, BF16), pltpu.VMEM((8, 16, 8, 2048), F32),
                        dma((8,)), dma((4,))],
        compiler_params=pltpu.CompilerParams(vmem_limit_bytes=LIMIT),
        name="last",
    )(g, e)


def on_device(samples, interp, translation, evaluate):
    by_box = samples.reshape(8, 2048, 128).transpose(1, 0, 2).reshape(8, 16, 16, 8, 128)
    state = main(by_box, interp, translation)
    return last(state, evaluate.transpose(0, 2, 1)).reshape(1024, 2048)


def solution(mesh):
    in_specs = (
        P(("gx", "gy"), None),
        P(None, ("gx", "gy"), None, None),
        P(None, None, ("gx", "gy"), None, None),
        P(None, ("gx", "gy"), None),
    )
    out_specs = P(None, ("gx", "gy"))
    return jax.shard_map(
        on_device, mesh=mesh, in_specs=in_specs, out_specs=out_specs, check_vma=False
    )
```

time: 399 us -> 132 us (0.33)
  waiting for transfers between devices: 277 us -> 0 us
  Pallas kernels: 0 us -> 131 us
  blocking collectives: 68 us -> 0 us
  matrix products: 31.9 us -> 0 us
  local copies, waits for them, and re-layouts: 12.6 us -> 0 us
  other arithmetic: 4.05 us -> 0 us
    ppermute x7 -> x0, waiting for transfers between devices: 277 us -> none  [partner_2(): return lax.ppermute(block, axis, route)]
    pallas_call x0 -> x2, Pallas kernels: none -> 131 us  [the longest x1 125 us: main(): pl.pallas_call(main_kernel, out_shape=jax.ShapeDtypeStruct((8, PARTS, 2,...]
    all_to_all x1 -> x0, blocking collectives: 68 us -> none  [on_device(): lax.all_to_all(samples, ('gx', 'gy'), split_axis=1, concat_axis=0, tiled=...]
    dot_general x29 -> x0, matrix products: 31.9 us -> none  [the longest x26 13.2 us: box_product(): jnp.einsum('bkj,bjr->bkr', weight, values, preferred_element_type=jnp.flo...]
    reshape x1 -> x0, local copies, waits for them, and re-layouts: 9.17 us -> none  [on_device(): return result.reshape(records, evaluate.shape[1])]
  transfers between devices with their start and end apart: 7 -> 0, of which waited for: 7 -> 0; matrix products, arithmetic and copies ran while one was open for 0% -> 0% of each run, Pallas kernels for 0% -> 0%
where the time goes in v5:
time: 132 us; the launch traced here: 131 us
  Pallas kernels  131 us (99%)
    pallas_call x1, Pallas kernels, main(): pl.pallas_call(main_kernel, out_shape=jax.ShapeDtypeStruct((8, PARTS, 2,...  125 us
    pallas_call x1, Pallas kernels, last(): pl.pallas_call(last_kernel, out_shape=jax.ShapeDtypeStruct((8, 16, 8, 204...  5.98 us

profile of v5, /device:TPU:1, one launch (start us, length us, event | category | flops | bytes accessed | tf_op | source)
XLA Modules:
  0.0 131.2 jit_solution(1653256443721454225)
XLA Ops:
  0.0 125.2 %levels.1.g_ref = bf16[8,4,2,2,2,32,128]{6,5,4,3,2,1,0:T(8,128)(2,1)} custom-call(bf16[8,16,16,8,128]{4,3,2,1,0:T(8,128)(2,1)} %bitcast.7, bf16[2,16,32,128]{3,2,1,0:T(8,128)(2,1)} %interp.1, bf16[7,2,16,32,64]{4,3,2,1,0:T(8,128)(2,1)} %translation.1), custom_call_target="tpu_custom_call" | custom-call | flops 2147483648 | bytes 10485760 | tf_op jit(solution)/shard_map/levels/pallas_call | solution.py:314
  125.2 6.0 %last.1 = f32[8,16,8,2048]{3,2,1,0:T(8,128)} custom-call(bf16[8,4,2,2,2,32,128]{6,5,4,3,2,1,0:T(8,128)(2,1)} %levels.1.g_ref, bf16[2,32,2048]{2,1,0:T(8,128)(2,1)} %bitcast.8), custom_call_target="tpu_custom_call" | custom-call | tf_op jit(solution)/shard_map/last/pallas_call | solution.py:385

commit v6 on v5

--- a/solution.py
+++ b/solution.py
@@ -28,6 +28,16 @@
 
 def q_of(z, e):
     return z if e == 0 else 3 - z
+
+
+def mixed(a, b):
+    order = []
+    for j in range(4):
+        order += [(a, 4 + j), (b, 4 + (j ^ 1)), (b, j ^ 2)]
+    return order
+
+
+X_ONLY = [(part, m) for part in (0, 1) for m in range(4)]
 
 
 def remote(src, dst, send, recv, device):
@@ -100,14 +110,22 @@
     lax.fori_loop(0, 16, pack, 0)
     pl.semaphore_wait(barrier, 31 + 3 + 64 - jnp.where(own_z, 1, 0))
 
-    def send_samples(part, those=range(8)):
+    def send_samples(part, m, rows):
         to = block_of(q ^ part, y)
-        for m in those:
-            src = samples.at[gx ^ m, :, pl.ds((q ^ part) * 4, 4)]
-            if m == 0 and part == 0:
-                pltpu.make_async_copy(src, x.at[part, gx], x_recv.at[part]).start()
-            else:
-                remote(src, x.at[part, gx], x_sent, x_recv.at[part], (gx ^ m, to)).start()
+        src = samples.at[gx ^ m, rows, pl.ds((q ^ part) * 4, 4)]
+        dst = x.at[part, gx, rows]
+        if m == 0 and part == 0:
+            pltpu.make_async_copy(src, dst, x_recv.at[part]).start()
+        else:
+            remote(src, dst, x_sent, x_recv.at[part], (gx ^ m, to)).start()
+
+    def burst(pieces, begin, end):
+        def each(h, carry):
+            for part, m in pieces:
+                send_samples(part, m, pl.ds(h * 4, 4))
+            return carry
+
+        lax.fori_loop(begin, end, each, 0)
 
     def own(i):
         beta = i ^ across
@@ -253,36 +271,15 @@
     own(1)
     own(2)
     own(3)
-    send_samples(0, (0, 1, 2, 3))
-    send_samples(1, (0, 1, 2, 3))
+    burst(X_ONLY, 0, 4)
     along_y(0)
-    send_samples(0, (4,))
-    send_samples(2, (5,))
-    send_samples(2, (2,))
-    send_samples(0, (5,))
-    send_samples(2, (4,))
-    send_samples(2, (3,))
+    burst(mixed(0, 2), 0, 2)
     along_y(1)
-    send_samples(0, (6,))
-    send_samples(2, (7,))
-    send_samples(2, (0,))
-    send_samples(0, (7,))
-    send_samples(2, (6,))
-    send_samples(2, (1,))
+    burst(mixed(0, 2), 2, 4)
     along_y(2)
-    send_samples(1, (4,))
-    send_samples(3, (5,))
-    send_samples(3, (2,))
-    send_samples(1, (5,))
-    send_samples(3, (4,))
-    send_samples(3, (3,))
+    burst(mixed(1, 3), 0, 2)
     along_y(3)
-    send_samples(1, (6,))
-    send_samples(3, (7,))
-    send_samples(3, (0,))
-    send_samples(1, (7,))
-    send_samples(3, (6,))
-    send_samples(3, (1,))
+    burst(mixed(1, 3), 2, 4)
     send_v()
     for step in range(PARTS + 2):
         if step < PARTS:

time: 132 us -> 122 us (0.924)
  Pallas kernels: 131 us -> 122 us
    pallas_call x1, Pallas kernels: 125 us -> 116 us  [main(): pl.pallas_call(main_kernel, out_shape=jax.ShapeDtypeStruct((8, PARTS, 2,...]
where the time goes in v6:
time: 122 us
  Pallas kernels  122 us (100%)
    pallas_call x1, Pallas kernels, main(): pl.pallas_call(main_kernel, out_shape=jax.ShapeDtypeStruct((8, PARTS, 2,...  116 us
    pallas_call x1, Pallas kernels, last(): pl.pallas_call(last_kernel, out_shape=jax.ShapeDtypeStruct((8, 16, 8, 204...  5.98 us

profile of v6, /device:TPU:1, one launch (start us, length us, event | category | flops | bytes accessed | tf_op | source)
XLA Modules:
  0.0 121.8 jit_solution(14803379279266601891)
XLA Ops:
  0.0 115.8 %levels.1.g_ref = bf16[8,4,2,2,2,32,128]{6,5,4,3,2,1,0:T(8,128)(2,1)} custom-call(bf16[8,16,16,8,128]{4,3,2,1,0:T(8,128)(2,1)} %bitcast.7, bf16[2,16,32,128]{3,2,1,0:T(8,128)(2,1)} %interp.1, bf16[7,2,16,32,64]{4,3,2,1,0:T(8,128)(2,1)} %translation.1), custom_call_target="tpu_custom_call" | custom-call | flops 2147483648 | bytes 10485760 | tf_op jit(solution)/shard_map/levels/pallas_call | solution.py:311
  115.8 6.0 %last.1 = f32[8,16,8,2048]{3,2,1,0:T(8,128)} custom-call(bf16[8,4,2,2,2,32,128]{6,5,4,3,2,1,0:T(8,128)(2,1)} %levels.1.g_ref, bf16[2,32,2048]{2,1,0:T(8,128)(2,1)} %bitcast.8), custom_call_target="tpu_custom_call" | custom-call | tf_op jit(solution)/shard_map/last/pallas_call | solution.py:382

commit v7 on v6

--- a/solution.py
+++ b/solution.py
@@ -273,9 +273,8 @@
     own(3)
     burst(X_ONLY, 0, 4)
     along_y(0)
-    burst(mixed(0, 2), 0, 2)
     along_y(1)
-    burst(mixed(0, 2), 2, 4)
+    burst(mixed(0, 2), 0, 4)
     along_y(2)
     burst(mixed(1, 3), 0, 2)
     along_y(3)
@@ -367,10 +366,10 @@
                 for side in range(2):
                     gy1 = block_of((k >> 1) ^ part, 2 * two + side)
                     r[:, gy1, :, at:at + 256] = got[side]
-        if k % 2 == 1:
-            wide = pl.ds(at - 256, 512)
+        if k % 2 == 1 or k == 6:
+            wide = pl.ds(at, 256) if k >= 6 else pl.ds(at - 256, 512)
             copy = pltpu.make_async_copy(
-                r.at[:, :, :, wide], r_ref.at[:, :, :, wide], store.at[k // 2])
+                r.at[:, :, :, wide], r_ref.at[:, :, :, wide], store.at[len(stores)])
             copy.start()
             stores.append(copy)
     for copy in stores:
@@ -385,7 +384,7 @@
         in_specs=[ANY, pl.BlockSpec(memory_space=pltpu.VMEM)],
         out_specs=ANY,
         scratch_shapes=[pltpu.VMEM(g.shape, BF16), pltpu.VMEM((8, 16, 8, 2048), F32),
-                        dma((8,)), dma((4,))],
+                        dma((8,)), dma((5,))],
         compiler_params=pltpu.CompilerParams(vmem_limit_bytes=LIMIT),
         name="last",
     )(g, e)

time: 122 us -> 122 us (level); the launches traced: 122 us -> 120 us
  Pallas kernels: 122 us -> 120 us
    pallas_call x1, Pallas kernels: 116 us -> 114 us  [main(): pl.pallas_call(main_kernel, out_shape=jax.ShapeDtypeStruct((8, PARTS, 2,...]
where the time goes in v7:
time: 122 us; the launch traced here: 120 us
  Pallas kernels  120 us (98%)
    pallas_call x1, Pallas kernels, main(): pl.pallas_call(main_kernel, out_shape=jax.ShapeDtypeStruct((8, PARTS, 2,...  114 us
    pallas_call x1, Pallas kernels, last(): pl.pallas_call(last_kernel, out_shape=jax.ShapeDtypeStruct((8, 16, 8, 204...  5.96 us

profile of v7, /device:TPU:1, one launch (start us, length us, event | category | flops | bytes accessed | tf_op | source)
XLA Modules:
  0.0 120.4 jit_solution(5579141288234193729)
XLA Ops:
  0.0 114.4 %levels.1.g_ref = bf16[8,4,2,2,2,32,128]{6,5,4,3,2,1,0:T(8,128)(2,1)} custom-call(bf16[8,16,16,8,128]{4,3,2,1,0:T(8,128)(2,1)} %bitcast.7, bf16[2,16,32,128]{3,2,1,0:T(8,128)(2,1)} %interp.1, bf16[7,2,16,32,64]{4,3,2,1,0:T(8,128)(2,1)} %translation.1), custom_call_target="tpu_custom_call" | custom-call | flops 2147483648 | bytes 10485760 | tf_op jit(solution)/shard_map/levels/pallas_call | solution.py:310
  114.4 6.0 %last.1 = f32[8,16,8,2048]{3,2,1,0:T(8,128)} custom-call(bf16[8,4,2,2,2,32,128]{6,5,4,3,2,1,0:T(8,128)(2,1)} %levels.1.g_ref, bf16[2,32,2048]{2,1,0:T(8,128)(2,1)} %bitcast.8), custom_call_target="tpu_custom_call" | custom-call | tf_op jit(solution)/shard_map/last/pallas_call | solution.py:381
